TPU v7x, 128 devices: a whole 4x4x4 slice. The times are simulated.
128 devices in a mesh: ctx: 16 (over y, z_lo, core), kv: 8 (over x, z_hi).
Axes of the slice: x: 4, y: 4, z: 4 (z_hi: 2, z_lo: 2; z = z_hi * 2 + z_lo), core: 2. Of those that a mesh axis runs over, the one named last changes fastest.
Arguments:
- prompt_in: bfloat16 [256, 8192], P(None, 'ctx'), may hold values from -6 to 6
- step_in: bfloat16 [3, 64, 8192], P(None, None, 'ctx'), may hold values from -6 to 6
- norm_gain: bfloat16 [8192], P('ctx'), may hold values from 0.099609375 to 1.8984375
- query_weight: bfloat16 [8192, 8192], P('ctx', 'kv'), may hold values from -0.125 to 0.125
- key_weight: bfloat16 [8192, 1024], P('ctx', 'kv'), may hold values from -0.125 to 0.125
- value_weight: bfloat16 [8192, 1024], P('ctx', 'kv'), may hold values from -0.0625 to 0.0625
- out_weight: bfloat16 [8192, 8192], P('kv', 'ctx'), may hold values from -0.125 to 0.125
- key_cache: bfloat16 [8, 131072, 128], P('kv', 'ctx'), may hold values from -540 to 540
- value_cache: bfloat16 [8, 131072, 128], P('kv', 'ctx'), may hold values from -5 to 5
- cache_lengths: int32 [16], P('ctx'), may hold values from 2048 to 8192
- visible: int32 [64], replicated, may hold values from 1 to 256, as said below
Outputs:
- prompt_out: bfloat16 [256, 8192], P('kv', 'ctx')
- step_out: bfloat16 [3, 64, 8192], P(None, 'kv', 'ctx')
Inputs may be any that keep to these rules, and one draw needn't show every extreme that they name: `visible`: prompt tokens seen by each decode row.
All inputs are finite; a program needn't handle non-finite values.
Results may differ from a plain program's by a relative error of at most 0.035.
Values may be sent and summed in bfloat16 or wider, within the bound.
A program may use at most 192 MiB of HBM per device.

v0:
```python
import jax
import jax.numpy as jnp
from jax import lax
from jax.sharding import PartitionSpec as P

D = 8192
HD = 128


EPSILON = 1e-05


def normalize_rows(inputs, norm_gain):
    widened = inputs.astype(jnp.float32)
    scaled = (widened * norm_gain.astype(jnp.float32)).astype(jnp.bfloat16)
    squares = jnp.sum(widened * widened, axis=-1)
    return (scaled, squares)


def shard_attention(queries, key_shard, value_shard, length, extra_pairs, extra_mask):
    flat_rows, head_size = queries.shape
    block_rows = 512
    blocks = flat_rows // block_rows
    extra_count = extra_pairs.shape[0]
    slots_live = lax.broadcasted_iota(jnp.int32, (1, key_shard.shape[0]), 1) < length
    extra_keys = extra_pairs[:, :head_size]
    extra_values = extra_pairs[:, head_size:]
    factor = head_size ** (-0.5)

    def one_block(operands):
        query_block, mask_block = operands
        cache_scores = (
            jnp.einsum("fd,cd->fc", query_block, key_shard, preferred_element_type=jnp.float32)
            * factor
        )
        extra_scores = (
            jnp.einsum("fd,ed->fe", query_block, extra_keys, preferred_element_type=jnp.float32)
            * factor
        )
        cache_scores = jnp.where(slots_live, cache_scores, -jnp.inf)
        extra_scores = jnp.where(mask_block, extra_scores, -jnp.inf)
        highest = jnp.maximum(jnp.max(cache_scores, axis=1), jnp.max(extra_scores, axis=1))
        cache_weights = jnp.exp(cache_scores - highest[:, None]).astype(jnp.bfloat16)
        extra_weights = jnp.exp(extra_scores - highest[:, None]).astype(jnp.bfloat16)
        totals = jnp.sum(cache_weights, axis=1, dtype=jnp.float32) + jnp.sum(
            extra_weights, axis=1, dtype=jnp.float32
        )
        mixture = jnp.dot(cache_weights, value_shard, preferred_element_type=jnp.float32)
        mixture = mixture + jnp.dot(extra_weights, extra_values, preferred_element_type=jnp.float32)
        return (highest, totals, mixture)

    highest, totals, mixture = lax.map(
        one_block,
        (
            queries.reshape(blocks, block_rows, head_size),
            extra_mask.reshape(blocks, block_rows, extra_count),
        ),
    )
    return (
        highest.reshape(flat_rows),
        totals.reshape(flat_rows),
        mixture.reshape(flat_rows, head_size),
    )


def run_section(
    inputs,
    limits,
    owner_rows,
    owner_steps,
    store_fn,
    stores,
    norm_gain,
    query_weight,
    pair_weight,
    out_weight,
    key_shard,
    value_shard,
    length,
):
    step_sets, row_count, _ = inputs.shape
    device_place = lax.axis_index("ctx")
    owned_rows = row_count // lax.axis_size("ctx")
    scaled, squares = normalize_rows(inputs, norm_gain)
    query_part = jnp.einsum("srd,de->sre", scaled, query_weight, preferred_element_type=jnp.float32)
    pair_part = jnp.einsum("srd,de->rse", scaled, pair_weight, preferred_element_type=jnp.float32)
    query_sum, square_sum = lax.psum((query_part, squares), "ctx")
    pair_sum = lax.psum_scatter(
        pair_part.astype(jnp.bfloat16), "ctx", scatter_dimension=0, tiled=True
    ).astype(jnp.float32)
    inverse = lax.rsqrt(square_sum / D + EPSILON)
    queries = (query_sum * inverse[:, :, None]).astype(jnp.bfloat16)
    own_inverse = jnp.swapaxes(
        lax.dynamic_slice_in_dim(inverse, device_place * owned_rows, owned_rows, 1), 0, 1
    )
    pair_rows = (pair_sum * own_inverse[:, :, None]).astype(jnp.bfloat16)
    prompt_pairs, own_pairs = store_fn(pair_rows, stores)
    extra_pairs = jnp.concatenate(
        [prompt_pairs, own_pairs.reshape(-1, own_pairs.shape[-1])], axis=0
    )
    prompt_own = prompt_pairs.shape[0]
    rows_own = own_pairs.shape[0]
    step_total = own_pairs.shape[1]
    prompt_index = device_place * prompt_own + lax.broadcasted_iota(
        jnp.int32, (1, 1, prompt_own), 2
    )
    seen_prompt = prompt_index < limits[:, :, None]
    slot_ids = lax.broadcasted_iota(jnp.int32, (1, 1, rows_own * step_total), 2)
    slot_row = device_place * rows_own + slot_ids // step_total
    slot_step = slot_ids % step_total
    seen_own = (slot_row == owner_rows[:, :, None]) & (slot_step <= owner_steps[:, :, None])
    seen_keys = jnp.concatenate([seen_prompt, seen_own], axis=2)
    heads_per = queries.shape[2] // HD
    extra_count = seen_keys.shape[2]
    extra_mask = jnp.broadcast_to(
        seen_keys[:, :, None, :], (step_sets, row_count, heads_per, extra_count)
    )
    extra_mask = extra_mask.reshape(step_sets * row_count * heads_per, extra_count)
    flat_queries = queries.reshape(step_sets * row_count * heads_per, HD)
    highest, totals, mixture = shard_attention(
        flat_queries, key_shard, value_shard, length, extra_pairs, extra_mask
    )
    overall = lax.pmax(highest, "ctx")
    rescale = jnp.exp(highest - overall)
    totals, mixture = (
        lax.psum((totals * rescale).astype(jnp.bfloat16), "ctx").astype(jnp.float32),
        lax.psum((mixture * rescale[:, None]).astype(jnp.bfloat16), "ctx").astype(jnp.float32),
    )
    attended = (mixture / totals[:, None]).astype(jnp.bfloat16)
    attended = attended.reshape(step_sets, row_count, heads_per * HD)
    my_share = lax.psum_scatter(
        jnp.einsum("srk,kd->rsd", attended, out_weight, preferred_element_type=jnp.float32).astype(
            jnp.bfloat16
        ),
        "kv",
        scatter_dimension=0,
        tiled=True,
    ).astype(jnp.float32)
    return (jnp.swapaxes(my_share, 0, 1).astype(jnp.bfloat16), (prompt_pairs, own_pairs))


def on_device(
    prompt_in,
    step_in,
    norm_gain,
    query_weight,
    key_weight,
    value_weight,
    out_weight,
    key_cache,
    value_cache,
    cache_lengths,
    visible,
):
    ctx_count = lax.axis_size("ctx")
    prompt_total = prompt_in.shape[0]
    row_total = visible.shape[0]
    step_total = step_in.shape[0]
    prompt_own = prompt_total // ctx_count
    rows_own = row_total // ctx_count
    pair_weight = jnp.concatenate([key_weight, value_weight], axis=1)
    pair_width = pair_weight.shape[1]
    shared = (
        norm_gain,
        query_weight,
        pair_weight,
        out_weight,
        key_cache[0],
        value_cache[0],
        cache_lengths[0],
    )
    stores = (
        jnp.zeros((prompt_own, pair_width), jnp.bfloat16),
        jnp.zeros((rows_own, step_total, pair_width), jnp.bfloat16),
    )

    def keep_prompt(pair_rows, current):
        return (pair_rows[:, 0, :], current[1])

    prompt_limits = lax.broadcasted_iota(jnp.int32, (1, prompt_total), 1) + 1
    nobody = jnp.full((1, prompt_total), -1, jnp.int32)
    prompt_out, stores = run_section(
        prompt_in[None], prompt_limits, nobody, nobody, keep_prompt, stores, *shared
    )
    row_ids = lax.broadcasted_iota(jnp.int32, (1, row_total), 1)
    outputs = []
    for step_index in range(step_total):

        def keep_one(pair_rows, current, step_index=step_index):
            return (
                current[0],
                lax.dynamic_update_slice_in_dim(current[1], pair_rows, step_index, 1),
            )

        step_ids = jnp.full((1, row_total), step_index, jnp.int32)
        result, stores = run_section(
            step_in[step_index : step_index + 1],
            visible[None, :],
            row_ids,
            step_ids,
            keep_one,
            stores,
            *shared
        )
        outputs.append(result)
    step_out = jnp.concatenate(outputs, axis=0)
    return (prompt_out[0], step_out)


def solution(mesh):
    placed = (
        P(None, "ctx"),
        P(None, None, "ctx"),
        P("ctx"),
        P("ctx", "kv"),
        P("ctx", "kv"),
        P("ctx", "kv"),
        P("kv", "ctx"),
        P("kv", "ctx", None),
        P("kv", "ctx", None),
        P("ctx"),
        P(),
    )
    return jax.shard_map(
        on_device,
        mesh=mesh,
        in_specs=placed,
        out_specs=(P("kv", "ctx"), P(None, "kv", "ctx")),
        check_vma=False,
    )
```

profile of v0, /device:TPU:0, one launch (start us, length us, event | category | flops | bytes accessed | tf_op | source)
XLA Modules:
  0.0 1040.7 jit_solution(12494352496434197446)
XLA Ops:
  27.3 31.0 %all-reduce.6 = (f32[1,256]{1,0:T(1,128)S(1)}, f32[1,64]{1,0:T(1,128)S(1)}, f32[1,64]{1,0:T(1,128)S(1)}, f32[1,64]{1,0:T(1,128)S(1)}) all-reduce(f32[1,256]{1,0:T(1,128)S(1)} %bitcast.209, f32[1,64]{1,0:T(1,128)S(1)} %bitcast.213, f32[1,64]{1,0:T(1,128)S(1)} %bitcast.212, ...), channel_id=1, replica_groups=mesh['ctx'=16,'kv'=8] {'ctx'}, use_global_device_ids=true, to_apply=%region_2.0 | all-reduce | flops 448 | bytes 3584 | tf_op jit(solution)/shard_map/psum | solution.py:87
  63.9 63.7 %all-reduce.21.cloned.1.call-done = (bf16[64,1,256]{2,0,1:T(8,128)(2,1)}, bf16[64,1,256]{2,0,1:T(8,128)(2,1)}, bf16[64,1,256]{2,0,1:T(8,128)(2,1)}) async-done(((bf16[64,1,256]{2,0,1:T(8,128)(2,1)}, bf16[64,1,256]{2,0,1:T(8,128)(2,1)}, bf16[64,1,256]{2,0,1:T(8,128)(2,1)}), (bf16[64,1,256]{2,0,1:T(8,128)(2,1)}, bf16[64,1,256]{2,0,1:T(8,128)(2,1)}, ...) | async-done | bytes 98320
  129.9 115.8 %all-reduce.17.cloned.1.call-done = bf16[256,1,256]{2,1,0:T(2,128)(2,1)} async-done(((bf16[256,1,256]{2,1,0:T(2,128)(2,1)}), bf16[256,1,256]{2,1,0:T(2,128)(2,1)}) %all-reduce.17.cloned.1.call-update) | async-done | bytes 131088
  246.5 126.1 %all-reduce.19.cloned.1.call-done = (f32[1,256,1024]{2,1,0:T(8,128)}, f32[1,64,1024]{2,1,0:T(8,128)}, f32[1,64,1024]{2,1,0:T(8,128)}, f32[1,64,1024]{2,1,0:T(8,128)}) async-done(((f32[1,256,1024]{2,1,0:T(8,128)}, f32[1,64,1024]{2,1,0:T(8,128)}, f32[1,64,1024]{2,1,0:T(8,128)}, f32[1,64,1024]{2,1,0:T(8,128)}), (f32[1,256,1024]{2,1,0:T(8,128)}, f32[1,64,1024]{2,1,0:T(8,128)}, f32[1,64,1024]{2,1,0:T(8,128)}, ...) | async-done | bytes 1835024 | tf_op jit(solution)/shard_map/psum | solution.py:87
  374.2 110.1 %while.3 = (s32[]{:T(128)}, f32[4,512]{1,0:T(4,128)S(1)}, f32[4,512]{1,0:T(4,128)S(1)}, f32[4,512,128]{2,1,0:T(8,128)}, bf16[4,512,128]{2,1,0:T(8,128)(2,1)S(1)}...) while((s32[]{:T(128)}, f32[4,512]{1,0:T(4,128)S(1)}, ...), condition=%wide.region_9.10_spmd.clone, body=%wide.region_4.9_spmd.clone.sunk | while | flops 2192774144 | bytes 64227508 | solution.py:52
  375.0 8.6 fusion.144
  383.9 11.2 %convert_reduce_fusion.10 = (f32[512]{0:T(512)S(1)}, bf16[512,8192]{1,0:T(8,128)(2,1)}) fusion(f32[512]{0:T(512)S(1)} %max.55, f32[512,8192]{1,0:T(8,128)} %get-tuple-element.411, pred[8192]{0:T(1024)(128)(4,1)S(1)} %compare_reduce_fusion.2), kind=kLoop, calls=%fused_computation.1.clone.1 | loop fusion | flops 25165312 | bytes 25178112 | tf_op jit(solution)/shard_map/while/body/eval_jaxpr/reduce_sum | solution.py:45
  402.5 8.6 fusion.144
  411.4 11.2 %convert_reduce_fusion.10 = (f32[512]{0:T(512)S(1)}, bf16[512,8192]{1,0:T(8,128)(2,1)}) fusion(f32[512]{0:T(512)S(1)} %max.55, f32[512,8192]{1,0:T(8,128)} %get-tuple-element.411, pred[8192]{0:T(1024)(128)(4,1)S(1)} %compare_reduce_fusion.2), kind=kLoop, calls=%fused_computation.1.clone.1 | loop fusion | flops 25165312 | bytes 25178112 | tf_op jit(solution)/shard_map/while/body/eval_jaxpr/reduce_sum | solution.py:45
  430.0 8.6 fusion.144
  438.9 11.2 %convert_reduce_fusion.10 = (f32[512]{0:T(512)S(1)}, bf16[512,8192]{1,0:T(8,128)(2,1)}) fusion(f32[512]{0:T(512)S(1)} %max.55, f32[512,8192]{1,0:T(8,128)} %get-tuple-element.411, pred[8192]{0:T(1024)(128)(4,1)S(1)} %compare_reduce_fusion.2), kind=kLoop, calls=%fused_computation.1.clone.1 | loop fusion | flops 25165312 | bytes 25178112 | tf_op jit(solution)/shard_map/while/body/eval_jaxpr/reduce_sum | solution.py:45
  457.6 8.6 fusion.144
  466.4 11.2 %convert_reduce_fusion.10 = (f32[512]{0:T(512)S(1)}, bf16[512,8192]{1,0:T(8,128)(2,1)}) fusion(f32[512]{0:T(512)S(1)} %max.55, f32[512,8192]{1,0:T(8,128)} %get-tuple-element.411, pred[8192]{0:T(1024)(128)(4,1)S(1)} %compare_reduce_fusion.2), kind=kLoop, calls=%fused_computation.1.clone.1 | loop fusion | flops 25165312 | bytes 25178112 | tf_op jit(solution)/shard_map/while/body/eval_jaxpr/reduce_sum | solution.py:45
  485.6 9.7 fusion.88
  495.4 8.1 fusion.86
  503.8 19.0 %fusion.13 = (f32[512]{0:T(512)S(1)}, f32[512]{0:T(512)S(1)}, f32[512]{0:T(512)S(1)}, f32[512,8192]{1,0:T(8,128)}) fusion(pred[8192]{0:T(1024)(128)(4,1)S(1)} %iota_compare_fusion.1, f32[512,8192]{1,0:T(8,128)} %fusion.88, f32[512,8192]{1,0:T(8,128)} %fusion.86, bf16[512,128]{1,0:T(8,128)(2,1)S(1)} %squeeze.45, bf16[1,8192,128]{2,1,0:T(8,128)(2,1)S(1)} %bitcast.197), kind=kOutput, calls=%fused_computation.29 | convolution fusion | flops 1111489024 | bytes 52574208 | tf_op jit(solution)/shard_map/while/body/eval_jaxpr/fd,cd->fc/dot_general | solution.py:33
  523.2 55.9 %all-reduce.8 = (f32[2048]{0:T(1024)S(1)}, f32[512]{0:T(512)S(1)}, f32[512]{0:T(512)S(1)}, f32[512]{0:T(512)S(1)}) all-reduce(f32[2048]{0:T(1024)S(1)} %bitcast.201, f32[512]{0:T(512)S(1)} %max.51, f32[512]{0:T(512)S(1)} %max.50, f32[512]{0:T(512)S(1)} %max.49), channel_id=1, replica_groups=mesh['ctx'=16,'kv'=8] {'ctx'}, use_global_device_ids=true, to_apply=%region_10.11 | all-reduce | flops 3584 | bytes 28672 | tf_op jit(solution)/shard_map/pmax | solution.py:123
  579.1 25.1 %convert_reduce_fusion.4 = (f32[512]{0:T(512)S(1)}, bf16[512,8192]{1,0:T(8,128)(2,1)S(1)}, f32[512]{0:T(512)S(1)}, bf16[512,8192]{1,0:T(8,128)(2,1)}, f32[512]{0:T(512)S(1)}, /*index=5*/bf16[512,8192]{1,0:T(8,128)(2,1)}) fusion(f32[512]{0:T(512)S(1)} %max.49, f32[512,8192]{1,0:T(8,128)} %get-tuple-element.321, pred[8192]{0:T(1024)(128)(4,1)S(1)} %iota_compare_fusion.1, ...), kind=kLoop, calls=%fused_computation.26 | loop fusion | flops 75495936 | bytes 75517952 | tf_op jit(solution)/shard_map/while/body/eval_jaxpr/reduce_sum | solution.py:45
  623.4 27.8 %all-reduce.9 = (bf16[2048]{0:T(1024)(128)(2,1)S(1)}, bf16[512]{0:T(512)(128)(2,1)S(1)}, bf16[512]{0:T(512)(128)(2,1)S(1)}, bf16[512]{0:T(512)(128)(2,1)S(1)}) all-reduce(bf16[2048]{0:T(1024)(128)(2,1)S(1)} %get-tuple-element.297, bf16[512]{0:T(512)(128)(2,1)S(1)} %get-tuple-element.293, ...), channel_id=1, replica_groups=mesh['ctx'=16,'kv'=8] {'ctx'}, use_global_device_ids=true, to_apply=%region_12.13 | all-reduce | flops 3584 | bytes 14336 | tf_op jit(solution)/shard_map/psum | solution.py:126
  651.3 90.8 %all-reduce.23.cloned.1.call-done = (bf16[2048,128]{1,0:T(8,128)(2,1)}, bf16[512,128]{1,0:T(8,128)(2,1)}, bf16[512,128]{1,0:T(8,128)(2,1)}, bf16[512,128]{1,0:T(8,128)(2,1)}) async-done(((bf16[2048,128]{1,0:T(8,128)(2,1)}, bf16[512,128]{1,0:T(8,128)(2,1)}, bf16[512,128]{1,0:T(8,128)(2,1)}, bf16[512,128]{1,0:T(8,128)(2,1)}), (bf16[2048,128]{1,0:T(8,128)(2,1)}, bf16[512,128]{1,0:T(8,128)(2,1)}, ...) | async-done | bytes 917520 | tf_op jit(solution)/shard_map/psum | solution.py:127
  751.1 65.1 %reduce-scatter.14.cloned.1.call-done = bf16[8,1,512]{2,0,1:T(8,128)(2,1)} async-done(((bf16[64,1,512]{2,0,1:T(8,128)(2,1)}), bf16[8,1,512]{2,0,1:T(8,128)(2,1)}) %reduce-scatter.14.cloned.1.call-update) | async-done | bytes 8208 | tf_op jit(solution)/shard_map/reduce_scatter | solution.py:131
  816.2 72.2 %reduce-scatter.12.cloned.1.call-done = bf16[8,1,512]{2,0,1:T(8,128)(2,1)} async-done(((bf16[64,1,512]{2,0,1:T(8,128)(2,1)}), bf16[8,1,512]{2,0,1:T(8,128)(2,1)}) %reduce-scatter.12.cloned.1.call-update) | async-done | bytes 8208 | tf_op jit(solution)/shard_map/reduce_scatter | solution.py:131
  888.4 72.3 %reduce-scatter.10.cloned.1.call-done = bf16[8,1,512]{2,0,1:T(8,128)(2,1)} async-done(((bf16[64,1,512]{2,0,1:T(8,128)(2,1)}), bf16[8,1,512]{2,0,1:T(8,128)(2,1)}) %reduce-scatter.10.cloned.1.call-update) | async-done | bytes 8208 | tf_op jit(solution)/shard_map/reduce_scatter | solution.py:131
  962.0 71.9 %reduce-scatter.8.cloned.1.call-done = bf16[32,1,512]{2,0,1:T(8,128)(2,1)} async-done(((bf16[256,1,512]{2,0,1:T(8,128)(2,1)}), bf16[32,1,512]{2,0,1:T(8,128)(2,1)}) %reduce-scatter.8.cloned.1.call-update) | async-done | bytes 32784 | tf_op jit(solution)/shard_map/reduce_scatter | solution.py:131
  (179 shorter events, 90.8 us)
Async XLA Ops:
  7.2 9.8 copy-start
  7.2 120.4 %all-reduce.21.cloned.1.call-start = ((), (), s32[]{:S(2)}) async-start(), calls=%async_computation.10 | async-start | bytes 196608
  14.7 231.0 %all-reduce.17.cloned.1.call-start = ((), (), s32[]{:S(2)}) async-start(), calls=%async_computation.8 | async-start | bytes 524288
  16.9 355.7 %all-reduce.19.cloned.1.call-start = ((), (), s32[]{:S(2)}) async-start(), calls=%async_computation.9 | async-start | bytes 3670016 | tf_op jit(solution)/shard_map/psum | solution.py:87
  25.0 717.0 %all-reduce.23.cloned.1.call-start = ((), (), s32[]{:S(2)}) async-start(), calls=%async_computation.11 | async-start | bytes 1835008 | tf_op jit(solution)/shard_map/psum | solution.py:127
  374.2 110.1 %copy-start.5 = (f32[1,64,1024]{2,1,0:T(8,128)S(1)}, f32[1,64,1024]{2,1,0:T(8,128)}, u32[]{:S(2)}) copy-start(f32[1,64,1024]{2,1,0:T(8,128)} %get-tuple-element.265) | copy-start | bytes 786436
  383.6 11.5 %copy-start.6 = (bf16[8192,128]{1,0:T(8,128)(2,1)S(1)}, bf16[8192,128]{1,0:T(8,128)(2,1)}, u32[]{:S(2)}) copy-start(bf16[8192,128]{1,0:T(8,128)(2,1)} %get-tuple-element.449) | copy-start | bytes 6291460 | tf_op jit(solution)/shard_map/while
  411.1 11.5 %copy-start.6 = (bf16[8192,128]{1,0:T(8,128)(2,1)S(1)}, bf16[8192,128]{1,0:T(8,128)(2,1)}, u32[]{:S(2)}) copy-start(bf16[8192,128]{1,0:T(8,128)(2,1)} %get-tuple-element.449) | copy-start | bytes 6291460 | tf_op jit(solution)/shard_map/while
  438.6 11.5 %copy-start.6 = (bf16[8192,128]{1,0:T(8,128)(2,1)S(1)}, bf16[8192,128]{1,0:T(8,128)(2,1)}, u32[]{:S(2)}) copy-start(bf16[8192,128]{1,0:T(8,128)(2,1)} %get-tuple-element.449) | copy-start | bytes 6291460 | tf_op jit(solution)/shard_map/while
  466.1 11.5 %copy-start.6 = (bf16[8192,128]{1,0:T(8,128)(2,1)S(1)}, bf16[8192,128]{1,0:T(8,128)(2,1)}, u32[]{:S(2)}) copy-start(bf16[8192,128]{1,0:T(8,128)(2,1)} %get-tuple-element.449) | copy-start | bytes 6291460 | tf_op jit(solution)/shard_map/while
  484.3 11.1 %copy-start.2 = (bf16[8192,128]{1,0:T(8,128)(2,1)S(1)}, bf16[8192,128]{1,0:T(8,128)(2,1)}, u32[]{:S(2)}) copy-start(bf16[8192,128]{1,0:T(8,128)(2,1)} %get-tuple-element.481) | copy-start | bytes 6291460
  485.6 17.8 %copy-start.4 = (f32[1,64,1024]{2,1,0:T(8,128)S(1)}, f32[1,64,1024]{2,1,0:T(8,128)}, u32[]{:S(2)}) copy-start(f32[1,64,1024]{2,1,0:T(8,128)} %get-tuple-element.266) | copy-start | bytes 786436
  579.1 25.1 %copy-start.7 = (bf16[8192,128]{1,0:T(8,128)(2,1)S(1)}, bf16[8192,128]{1,0:T(8,128)(2,1)}, u32[]{:S(2)}) copy-start(bf16[8192,128]{1,0:T(8,128)(2,1)} %get-tuple-element.524) | copy-start | bytes 6291460
  610.0 134.8 %copy-start.3 = (bf16[1024,512]{1,0:T(8,128)(2,1)S(1)}, bf16[1024,512]{1,0:T(8,128)(2,1)}, u32[]{:S(2)}) copy-start(bf16[1024,512]{1,0:T(8,128)(2,1)} %param.19) | copy-start | bytes 3145732
  610.0 423.9 %copy-start.1 = (bf16[512,1024]{1,0:T(8,128)(2,1)S(1)}, bf16[512,1024]{1,0:T(8,128)(2,1)}, u32[]{:S(2)}) copy-start(bf16[512,1024]{1,0:T(8,128)(2,1)} %param.16) | copy-start | bytes 3145732
  623.4 192.8 %reduce-scatter.14.cloned.1.call-start = ((), (), s32[]{:S(2)}) async-start(), calls=%async_computation.7 | async-start | bytes 73728 | tf_op jit(solution)/shard_map/reduce_scatter | solution.py:131
  745.7 142.7 %reduce-scatter.12.cloned.1.call-start = ((), (), s32[]{:S(2)}) async-start(), calls=%async_computation.6 | async-start | bytes 73728 | tf_op jit(solution)/shard_map/reduce_scatter | solution.py:131
  748.9 211.7 %reduce-scatter.10.cloned.1.call-start = ((), (), s32[]{:S(2)}) async-start(), calls=%async_computation.5 | async-start | bytes 73728 | tf_op jit(solution)/shard_map/reduce_scatter | solution.py:131
  749.9 283.9 %reduce-scatter.8.cloned.1.call-start = ((), (), s32[]{:S(2)}) async-start(), calls=%async_computation.4 | async-start | bytes 294912 | tf_op jit(solution)/shard_map/reduce_scatter | solution.py:131
Sparse Core Ops, SparseCore 0:
  14.9 112.6 all-reduce.20
  130.2 115.4 all-reduce.16
  248.5 124.1 all-reduce.18
  623.5 118.4 all-reduce.22
  745.8 70.3 reduce-scatter.13
  819.6 68.7 reduce-scatter.11
  891.9 68.6 reduce-scatter.9
  964.8 69.0 reduce-scatter.7
where the time goes:
time: 1040 us
  waiting for transfers between devices  678 us (65%)
  matrix products  133 us (13%)
  blocking collectives  115 us (11%)
  other arithmetic  90.4 us (9%)
  between operations  16.3 us (2%)
    reduce_scatter x4, waiting for transfers between devices, run_section(): lax.psum_scatter(jnp.einsum('srk,kd->rsd', attended, out_weight, preferre...  281 us
    unnamed x10, waiting for transfers between devices  180 us
    psum x1, waiting for transfers between devices, run_section(): query_sum, square_sum = lax.psum((query_part, squares), 'ctx')  126 us
    psum x1, waiting for transfers between devices, run_section(): lax.psum((mixture * rescale[:, None]).astype(jnp.bfloat16), 'ctx')  90.8 us
    dot_general x7, matrix products, one_block(): jnp.einsum('fd,cd->fc', query_block, key_shard, preferred_element_type=jn...  71.2 us
    reduce_sum x5, other arithmetic, one_block(): jnp.sum(cache_weights, axis=1, dtype=jnp.float32)  69.8 us
    pmax x1, blocking collectives, run_section(): overall = lax.pmax(highest, 'ctx')  55.9 us
    dot_general x7, matrix products, one_block(): jnp.dot(cache_weights, value_shard, preferred_element_type=jnp.float32)  36.7 us
  transfers between devices with their start and end apart: 8, of which 8 were waited for; matrix products, arithmetic and copies ran while one was open for 2% of the time, Pallas kernels for 0%

commit v1 on v0

v1 whole, which is shorter than its diff:
```python
import jax
import jax.numpy as jnp
from jax import lax
from jax.experimental import pallas as pl
from jax.experimental.pallas import tpu as pltpu
from jax.sharding import PartitionSpec as P

D = 8192
HD = 128
EPSILON = 1e-05
MESH = pl.DeviceIdType.MESH
F32 = jnp.float32
BF16 = jnp.bfloat16

CTX = 16
KV = 8
CHIPS = 8
GROUP = 56
PROMPT_G = 32
ROWS_G = 8
STEPS = 3
ALL = CHIPS * GROUP
FEAT = 512
PARTS = 2
WIDE = 512 // PARTS
HEADS_P = WIDE // HD
FLAT = HEADS_P * GROUP
BLOCK = 4 * FLAT
SLOTS = 8192
TILE = 512
TILES = SLOTS // TILE
LOG2E = 1.4426950408889634
HIDDEN = -1e30


def kernel(
    prompt_ref,
    step_ref,
    gain_ref,
    wq_hbm,
    wk_hbm,
    wv_hbm,
    wo_hbm,
    key_hbm,
    value_hbm,
    length_ref,
    visible_ref,
    prompt_out,
    step_out,
    x_raw,
    gain,
    xs,
    wq,
    wkv,
    wo,
    k_raw,
    k_t,
    v_x,
    kx_t,
    vx_x,
    bias,
    inv,
    po,
    kvp,
    a0_send,
    a0_recv,
    kv0_send,
    kv0_recv,
    sq0_send,
    sq0_recv,
    a1_send,
    a1_recv,
    kv1_send,
    kv1_recv,
    sq1_send,
    sq1_recv,
    q_all,
    s_buf,
    sx_buf,
    mx,
    own_mix,
    own_row,
    b0_send,
    b0_recv,
    b1_send,
    b1_recv,
    att,
    o_acc,
    c_send,
    c_recv,
    load_sem,
    p_send,
    p_recv,
    a1_ss,
    a1_rs,
    kv1_ss,
    kv1_rs,
    sq1_ss,
    sq1_rs,
    qg_ss,
    qg_rs,
    qf_ss,
    qf_rs,
    b1_ss,
    b1_rs,
    ag_ss,
    ag_rs,
    af_ss,
    af_rs,
    c_ss,
    c_rs,
):
    c = lax.axis_index("ctx")
    k = lax.axis_index("kv")
    core = lax.rem(c, 2)
    j = lax.div(c, 2)
    other = 1 - core
    sib = (c + 1 - 2 * core, k)

    def chip(jt):
        return (2 * jt + core, k)

    def away(d):
        return lax.rem(j + d, CHIPS)

    def remote(src, dst, ss, rs, dev):
        return pltpu.make_async_remote_copy(
            src_ref=src, dst_ref=dst, send_sem=ss, recv_sem=rs, device_id=dev, device_id_type=MESH
        )

    loads = [pltpu.make_async_copy(prompt_ref, x_raw.at[:, 0:PROMPT_G], load_sem.at[0])]
    for s in range(STEPS):
        low = PROMPT_G + s * ROWS_G
        loads.append(
            pltpu.make_async_copy(step_ref.at[s], x_raw.at[:, low : low + ROWS_G], load_sem.at[1 + s])
        )
    loads.append(pltpu.make_async_copy(gain_ref, gain, load_sem.at[4]))
    loads.append(pltpu.make_async_copy(wq_hbm, wq, load_sem.at[5]))
    loads.append(pltpu.make_async_copy(wk_hbm, wkv.at[:, 0:HD], load_sem.at[6]))
    loads.append(pltpu.make_async_copy(wv_hbm, wkv.at[:, HD : 2 * HD], load_sem.at[7]))
    key_load = pltpu.make_async_copy(key_hbm, k_raw, load_sem.at[8])
    value_load = pltpu.make_async_copy(value_hbm, v_x.at[:, 0:HD], load_sem.at[9])
    wo_load = pltpu.make_async_copy(wo_hbm, wo, load_sem.at[10])
    for copy in loads:
        copy.start()
    key_load.start()
    value_load.start()
    wo_load.start()

    barrier = pltpu.get_barrier_semaphore()
    pl.semaphore_signal(barrier, inc=1, device_id=sib, device_id_type=MESH)
    for d in range(1, CHIPS):
        pl.semaphore_signal(barrier, inc=1, device_id=chip(away(d)), device_id_type=MESH)
        pl.semaphore_signal(
            barrier, inc=1, device_id=(c, lax.rem(k + d, KV)), device_id_type=MESH
        )

    eye_flat = lax.broadcasted_iota(jnp.int32, (FLAT, HD), 0) == lax.broadcasted_iota(
        jnp.int32, (FLAT, HD), 1
    )
    eye_group = lax.broadcasted_iota(jnp.int32, (GROUP, HD), 0) == lax.broadcasted_iota(
        jnp.int32, (GROUP, HD), 1
    )

    def as_row(eye, column):
        return jnp.sum(jnp.where(eye, column, 0.0), axis=0, keepdims=True)

    def as_column(eye, row):
        return jnp.sum(jnp.where(eye, row, 0.0), axis=1, keepdims=True)

    for copy in loads:
        copy.wait()
    xf = x_raw[...].astype(F32).reshape(ALL, FEAT)
    xs[...] = (xf * gain[...].astype(F32)).astype(BF16)
    squares = jnp.sum(xf * xf, axis=1, keepdims=True)
    for g in range(CHIPS):
        sq0_send[g] = as_row(eye_group, squares[g * GROUP : (g + 1) * GROUP])
    pl.semaphore_wait(barrier, 2 * CHIPS - 1)

    def first(p):
        return remote(a0_send.at[p], a0_recv.at[p], p_send.at[p], p_recv.at[p], sib)

    def project(column):
        return jnp.dot(
            xs[...], wq[:, pl.ds(pl.multiple_of(column, HD), WIDE)], preferred_element_type=F32
        )

    kv_first = remote(kv0_send, kv0_recv, p_send.at[PARTS], p_recv.at[PARTS], sib)
    sq_first = remote(sq0_send, sq0_recv, p_send.at[PARTS + 1], p_recv.at[PARTS + 1], sib)
    sq_first.start()
    for p in range(PARTS):
        a0_send[p] = project(other * 512 + p * WIDE).astype(BF16)
        first(p).start()
        if p == 0:
            pairs = jnp.dot(xs[...], wkv[...], preferred_element_type=F32)
            pairs = pairs.reshape(CHIPS, GROUP, 2 * HD)
            of_prompt = pairs[:, 0:PROMPT_G]
            of_steps = jnp.concatenate(
                [pairs[:, PROMPT_G:], jnp.zeros((CHIPS, 8, 2 * HD), F32)], axis=1
            )
            kv0_send[...] = jnp.where(core == 0, of_steps, of_prompt).astype(BF16)
            kv_first.start()
            kvp[...] = jnp.where(core == 0, of_prompt, of_steps)
        po[p] = project(core * 512 + p * WIDE)

    length = length_ref[0]

    def prepare_keys(t, carry):
        low = pl.multiple_of(t * TILE, TILE)
        live = (lax.broadcasted_iota(jnp.int32, (TILE, HD), 0) + low) < length
        keys = jnp.where(live, k_raw[pl.ds(low, TILE)].astype(F32), k_raw[0:1].astype(F32))
        k_t[:, pl.ds(low, TILE)] = keys.astype(BF16).T
        return carry

    def prepare_values(t, carry):
        low = pl.multiple_of(t * TILE, TILE)
        live = (lax.broadcasted_iota(jnp.int32, (TILE, HD), 0) + low) < length
        v_x[pl.ds(low, TILE), 0:HD] = jnp.where(
            live, v_x[pl.ds(low, TILE), 0:HD].astype(F32), 0.0
        ).astype(BF16)
        v_x[pl.ds(low, TILE), HD : 2 * HD] = jnp.where(live, 1.0, 0.0).astype(BF16)
        return carry

    def a1_copy(p, jt, slot):
        return remote(
            a1_send.at[p, jt], a1_recv.at[p, slot], a1_ss.at[p, jt], a1_rs.at[p, slot], chip(jt)
        )

    def kv1_copy(jt, slot):
        return remote(kv1_send.at[jt], kv1_recv.at[slot], kv1_ss.at[jt], kv1_rs.at[slot], chip(jt))

    def sq1_copy(jt, slot):
        return remote(sq1_send.at[jt], sq1_recv.at[slot], sq1_ss.at[jt], sq1_rs.at[slot], chip(jt))

    def spread(p):
        first(p).wait_recv()
        total = po[p] + a0_recv[p].astype(F32)
        a1_send[p] = total.reshape(CHIPS, GROUP, WIDE).astype(BF16)
        for d in range(1, CHIPS):
            a1_copy(p, away(d), j).start()

    def spread_small():
        sq_first.wait_recv()
        sq1_send[...] = sq0_send[...] + sq0_recv[...]
        kv_first.wait_recv()
        kv1_send[...] = (kvp[...] + kv0_recv[...].astype(F32)).astype(BF16)
        for d in range(1, CHIPS):
            sq1_copy(away(d), j).start()
            kv1_copy(away(d), j).start()

    def small_sums():
        square = sq1_send[j]
        for d in range(1, CHIPS):
            src = away(d)
            sq1_copy(src, src).wait_recv()
            square = square + sq1_recv[src]
        inverse = lax.rsqrt(square / D + EPSILON)
        inv[...] = jnp.broadcast_to(as_column(eye_group, inverse), (GROUP, HD))

    def pair_sums():
        pair = kv1_send[j].astype(F32)
        for d in range(1, CHIPS):
            src = away(d)
            kv1_copy(src, src).wait_recv()
            pair = pair + kv1_recv[src].astype(F32)
        inv_steps = jnp.concatenate([inv[PROMPT_G:], jnp.zeros((8, HD), F32)], axis=0)
        scale = jnp.where(core == 0, inv[0:PROMPT_G], inv_steps)
        blank = jnp.zeros((HD - PROMPT_G, HD), F32)
        new_keys = jnp.concatenate([pair[:, 0:HD] * scale, blank], axis=0)
        new_values = jnp.concatenate([pair[:, HD:] * scale, blank], axis=0)
        kx_t[...] = new_keys.T.astype(BF16)
        vx_x[:, 0:HD] = new_values.astype(BF16)
        vx_x[:, HD : 2 * HD] = jnp.ones((HD, HD), BF16)

    def q_copy(p, jt, slot):
        return remote(
            q_all.at[p, core, slot],
            q_all.at[p, core, slot],
            qg_ss.at[p, jt],
            qg_rs.at[p, slot],
            chip(jt),
        )

    def q_forward(p, column, slot):
        return remote(
            q_all.at[p, column, slot],
            q_all.at[p, column, slot],
            qf_ss.at[p, slot],
            qf_rs.at[p, slot],
            sib,
        )

    def query_sums(p):
        total = a1_send[p, j].astype(F32)
        for d in range(1, CHIPS):
            src = away(d)
            a1_copy(p, src, src).wait_recv()
            total = total + a1_recv[p, src].astype(F32)
        scale = inv[...] * (HD**-0.5 * LOG2E)
        flat = jnp.concatenate(
            [total[:, h * HD : (h + 1) * HD] * scale for h in range(HEADS_P)], axis=0
        )
        q_all[p, core, j] = flat.astype(BF16)
        for d in range(1, CHIPS):
            q_copy(p, away(d), j).start()
        q_forward(p, core, j).start()

    def forward_queries(p):
        for d in range(1, CHIPS):
            src = away(d)
            q_copy(p, src, src).wait_recv()
            q_forward(p, core, src).start()

    def await_queries(p):
        for slot in range(CHIPS):
            q_forward(p, other, slot).wait_recv()

    def prepare_bias():
        lane = lax.broadcasted_iota(jnp.int32, (GROUP, HD), 1)
        sub = lax.broadcasted_iota(jnp.int32, (GROUP, HD), 0)
        sub8 = lax.broadcasted_iota(jnp.int32, (ROWS_G, HD), 0)
        position = j * PROMPT_G + lane
        key_row = j * ROWS_G + lax.rem(lane, ROWS_G)
        key_step = lax.div(lane, ROWS_G)
        past = sub - PROMPT_G
        is_step = past >= 0
        query_step = lax.div(jnp.maximum(past, 0), ROWS_G)
        for g in range(CHIPS):
            seen_by_row = jnp.zeros((ROWS_G, HD), jnp.int32)
            for b in range(ROWS_G):
                seen_by_row = jnp.where(sub8 == b, visible_ref[g * ROWS_G + b], seen_by_row)
            by_row = jnp.concatenate(
                [jnp.zeros((PROMPT_G, HD), jnp.int32)] + [seen_by_row] * STEPS, axis=0
            )
            limit = jnp.where(is_step, by_row, g * PROMPT_G + sub + 1)
            query_row = g * ROWS_G + lax.rem(jnp.maximum(past, 0), ROWS_G)
            score_prompt = jnp.where((lane < PROMPT_G) & (position < limit), 0.0, HIDDEN)
            score_steps = jnp.where(
                (lane < STEPS * ROWS_G)
                & is_step
                & (key_row == query_row)
                & (key_step <= query_step),
                0.0,
                HIDDEN,
            )
            both = jnp.where(core == 0, score_prompt, score_steps)
            bias[g] = jnp.concatenate([both] * HEADS_P, axis=0)

    key_load.wait()
    lax.fori_loop(0, TILES // 2, prepare_keys, 0)
    spread(0)
    spread_small()
    prepare_bias()
    lax.fori_loop(TILES // 2, TILES, prepare_keys, 0)
    spread(1)
    small_sums()
    query_sums(0)
    pair_sums()
    value_load.wait()
    lax.fori_loop(0, TILES, prepare_values, 0)
    forward_queries(0)

    def place(n):
        p = lax.div(n, 4)
        part = lax.rem(n, 4)
        mine = lax.rem(p + lax.div(part, 2), 2) == 0
        return p, jnp.where(mine, core, other), lax.rem(part, 2), mine

    def lane_max(scores):
        high = scores[:, 0:HD]
        for u in range(1, scores.shape[1] // HD):
            high = jnp.maximum(high, scores[:, u * HD : (u + 1) * HD])
        return high

    def sweep(n_scores, top):
        if n_scores is not None:
            p, column, half, _ = place(n_scores)
            queries = q_all[p, column, pl.ds(half * 4, 4)].reshape(BLOCK, HD)
            mask = bias[pl.ds(half * 4, 4)].reshape(BLOCK, HD)
        high = None
        mixed = None
        for t in range(TILES + 1):
            cols = slice(t * TILE, (t + 1) * TILE)
            if top is not None:
                old = s_buf[t] if t < TILES else sx_buf[...]
                weights = jnp.exp2(old - top).astype(BF16)
            if n_scores is not None:
                if t < TILES:
                    scores = jnp.dot(queries, k_t[:, cols], preferred_element_type=F32)
                    s_buf[t] = scores
                else:
                    scores = jnp.dot(queries, kx_t[...], preferred_element_type=F32) + mask
                    sx_buf[...] = scores
                peak = lane_max(scores)
                high = peak if high is None else jnp.maximum(high, peak)
            if top is not None:
                values = v_x[cols] if t < TILES else vx_x[...]
                part = jnp.dot(weights, values, preferred_element_type=F32)
                mixed = part if mixed is None else mixed + part
        if n_scores is not None:
            mx[...] = high
        return mixed

    def split3(row):
        one = row.astype(BF16).astype(F32)
        two = (row - one).astype(BF16).astype(F32)
        return one, two, row - one - two

    def packed(mixture, top_row, total_row):
        sub = lax.broadcasted_iota(jnp.int32, (16, HD), 0)
        stats = jnp.zeros((16, HD), F32)
        for i, piece in enumerate(split3(top_row) + split3(total_row)):
            stats = jnp.where(sub == i, piece, stats)
        return jnp.concatenate([mixture, stats], axis=0).astype(BF16)

    def unpacked(packet):
        wide = packet.astype(F32)
        stats = wide[FLAT:]
        return (
            wide[0:FLAT],
            stats[0:1] + stats[1:2] + stats[2:3],
            stats[3:4] + stats[4:5] + stats[5:6],
        )

    def keep(n, mixed, top):
        p, _, half, mine = place(n)
        for i in range(4):
            rows = slice(i * FLAT, (i + 1) * FLAT)
            top_row = as_row(eye_flat, top[rows])
            total_row = as_row(eye_flat, mixed[rows, HD:])

            @pl.when(mine)
            def _():
                own_mix[p, half * 4 + i] = mixed[rows, 0:HD]
                own_row[p, half * 4 + i, 0:1] = top_row
                own_row[p, half * 4 + i, 1:2] = total_row

            @pl.when(jnp.logical_not(mine))
            def _():
                b0_send[p, half * 4 + i] = packed(mixed[rows, 0:HD], top_row, total_row)

    def b0_copy(p):
        return remote(
            b0_send.at[p], b0_recv.at[p], p_send.at[PARTS + 2 + p], p_recv.at[PARTS + 2 + p], sib
        )

    def b1_copy(p, jt, slot):
        return remote(
            b1_send.at[p, jt], b1_recv.at[p, slot], b1_ss.at[p, jt], b1_rs.at[p, slot], chip(jt)
        )

    def merge_pair(p, half):
        for i in range(4):
            jt = half * 4 + i
            mix1, top1, tot1 = unpacked(b0_recv[p, jt])
            top0 = own_row[p, jt, 0:1]
            tot0 = own_row[p, jt, 1:2]
            top = jnp.maximum(top0, top1)
            w0 = jnp.exp2(top0 - top)
            w1 = jnp.exp2(top1 - top)
            mixture = own_mix[p, jt] * as_column(eye_flat, w0) + mix1 * as_column(eye_flat, w1)
            b1_send[p, jt] = packed(mixture, top, w0 * tot0 + w1 * tot1)

            @pl.when(jt != j)
            def _():
                b1_copy(p, jt, j).start()

    def att_copy(p, jt, slot):
        return remote(
            att.at[p, core, slot], att.at[p, core, slot], ag_ss.at[p, jt], ag_rs.at[p, slot], chip(jt)
        )

    def att_forward(p, column, slot):
        return remote(
            att.at[p, column, slot], att.at[p, column, slot], af_ss.at[p, slot], af_rs.at[p, slot], sib
        )

    def merge_all(p):
        pieces = [unpacked(b1_send[p, j])]
        for d in range(1, CHIPS):
            src = away(d)
            b1_copy(p, src, src).wait_recv()
            pieces.append(unpacked(b1_recv[p, src]))
        top = pieces[0][1]
        for piece in pieces[1:]:
            top = jnp.maximum(top, piece[1])
        shares = [jnp.exp2(piece[1] - top) for piece in pieces]
        total = shares[0] * pieces[0][2]
        for share, piece in zip(shares[1:], pieces[1:]):
            total = total + share * piece[2]
        result = jnp.zeros((FLAT, HD), F32)
        for share, piece in zip(shares, pieces):
            result = result + piece[0] * as_column(eye_flat, share)
        result = result * as_column(eye_flat, 1.0 / total)
        att[p, core, j] = jnp.concatenate(
            [result[h * GROUP : (h + 1) * GROUP] for h in range(HEADS_P)], axis=1
        ).astype(BF16)
        for d in range(1, CHIPS):
            att_copy(p, away(d), j).start()
        att_forward(p, core, j).start()

    def forward_attended(p):
        for d in range(1, CHIPS):
            src = away(d)
            att_copy(p, src, src).wait_recv()
            att_forward(p, core, src).start()

    def await_attended(p):
        for slot in range(CHIPS):
            att_forward(p, other, slot).wait_recv()

    def out_part(p, column):
        rows = att[p, column].astype(F32).reshape(ALL, WIDE).astype(BF16)
        low = pl.multiple_of(column * 512 + p * WIDE, WIDE)
        return jnp.dot(rows, wo[pl.ds(low, WIDE)], preferred_element_type=F32)

    def step_top():
        return jnp.max(mx[...], axis=1, keepdims=True)

    sweep(0, None)

    def step(n, carry):
        @pl.when(n == 1)
        def _():
            await_queries(0)
            query_sums(1)

        @pl.when(n == 2)
        def _():
            forward_queries(1)

        @pl.when(n == 3)
        def _():
            await_queries(1)

        @pl.when(n == 4)
        def _():
            b0_copy(0).start()

        @pl.when(n == 5)
        def _():
            b0_copy(0).wait_recv()
            merge_pair(0, 0)
            merge_pair(0, 1)

        @pl.when(n == 6)
        def _():
            b0_copy(1).start()
            merge_all(0)

        top = step_top()
        mixed = sweep(n + 1, top)
        keep(n, mixed, jnp.broadcast_to(top, (BLOCK, HD)))
        return carry

    lax.fori_loop(0, 7, step, 0)
    forward_attended(0)
    b0_copy(1).wait_recv()
    merge_pair(1, 0)
    top = step_top()
    mixed = sweep(None, top)
    keep(7, mixed, jnp.broadcast_to(top, (BLOCK, HD)))
    merge_pair(1, 1)
    await_attended(0)
    wo_load.wait()
    o_acc[...] = out_part(0, 0) + out_part(0, 1)
    merge_all(1)
    forward_attended(1)
    o_acc[...] += out_part(1, core)
    await_attended(1)
    result = o_acc[...] + out_part(1, other)

    def c_copy(kt, slot):
        return remote(c_send.at[kt], c_recv.at[slot], c_ss.at[kt], c_rs.at[slot], (c, kt))

    c_send[...] = result.reshape(KV, GROUP, FEAT).astype(BF16)
    for d in range(1, KV):
        c_copy(lax.rem(k + d, KV), k).start()
    final = c_send[k].astype(F32)
    for d in range(1, KV):
        src = lax.rem(k + d, KV)
        c_copy(src, src).wait_recv()
        final = final + c_recv[src].astype(F32)
    prompt_out[...] = final[0:PROMPT_G].astype(BF16)
    for s in range(STEPS):
        low = PROMPT_G + s * ROWS_G
        step_out[s] = final[low : low + ROWS_G].astype(BF16)

    kv_first.wait_send()
    sq_first.wait_send()
    for p in range(PARTS):
        first(p).wait_send()
        b0_copy(p).wait_send()
        for slot in range(CHIPS):
            q_forward(p, core, slot).wait_send()
            att_forward(p, core, slot).wait_send()
    for d in range(1, CHIPS):
        jt = away(d)
        sq1_copy(jt, j).wait_send()
        kv1_copy(jt, j).wait_send()
        c_copy(lax.rem(k + d, KV), k).wait_send()
        for p in range(PARTS):
            a1_copy(p, jt, j).wait_send()
            q_copy(p, jt, j).wait_send()
            b1_copy(p, jt, j).wait_send()
            att_copy(p, jt, j).wait_send()


def on_device(
    prompt_in,
    step_in,
    norm_gain,
    query_weight,
    key_weight,
    value_weight,
    out_weight,
    key_cache,
    value_cache,
    cache_lengths,
    visible,
):
    dma = pltpu.SemaphoreType.DMA
    hbm = pl.BlockSpec(memory_space=pl.ANY)
    smem = pl.BlockSpec(memory_space=pltpu.SMEM)
    vmem = pl.BlockSpec(memory_space=pltpu.VMEM)
    scratch = [
        pltpu.VMEM((CHIPS, GROUP, FEAT), BF16),
        pltpu.VMEM((1, FEAT), BF16),
        pltpu.VMEM((ALL, FEAT), BF16),
        pltpu.VMEM((FEAT, 1024), BF16),
        pltpu.VMEM((FEAT, 2 * HD), BF16),
        pltpu.VMEM((1024, FEAT), BF16),
        pltpu.VMEM((SLOTS, HD), BF16),
        pltpu.VMEM((HD, SLOTS), BF16),
        pltpu.VMEM((SLOTS, 2 * HD), BF16),
        pltpu.VMEM((HD, HD), BF16),
        pltpu.VMEM((HD, 2 * HD), BF16),
        pltpu.VMEM((CHIPS, FLAT, HD), F32),
        pltpu.VMEM((GROUP, HD), F32),
        pltpu.VMEM((PARTS, ALL, WIDE), F32),
        pltpu.VMEM((CHIPS, PROMPT_G, 2 * HD), F32),
        pltpu.VMEM((PARTS, ALL, WIDE), BF16),
        pltpu.VMEM((PARTS, ALL, WIDE), BF16),
        pltpu.VMEM((CHIPS, PROMPT_G, 2 * HD), BF16),
        pltpu.VMEM((CHIPS, PROMPT_G, 2 * HD), BF16),
        pltpu.VMEM((CHIPS, 1, HD), F32),
        pltpu.VMEM((CHIPS, 1, HD), F32),
        pltpu.VMEM((PARTS, CHIPS, GROUP, WIDE), BF16),
        pltpu.VMEM((PARTS, CHIPS, GROUP, WIDE), BF16),
        pltpu.VMEM((CHIPS, PROMPT_G, 2 * HD), BF16),
        pltpu.VMEM((CHIPS, PROMPT_G, 2 * HD), BF16),
        pltpu.VMEM((CHIPS, 1, HD), F32),
        pltpu.VMEM((CHIPS, 1, HD), F32),
        pltpu.VMEM((PARTS, 2, CHIPS, FLAT, HD), BF16),
        pltpu.VMEM((TILES, BLOCK, TILE), F32),
        pltpu.VMEM((BLOCK, HD), F32),
        pltpu.VMEM((BLOCK, HD), F32),
        pltpu.VMEM((PARTS, CHIPS, FLAT, HD), F32),
        pltpu.VMEM((PARTS, CHIPS, 8, HD), F32),
        pltpu.VMEM((PARTS, CHIPS, FLAT + 16, HD), BF16),
        pltpu.VMEM((PARTS, CHIPS, FLAT + 16, HD), BF16),
        pltpu.VMEM((PARTS, CHIPS, FLAT + 16, HD), BF16),
        pltpu.VMEM((PARTS, CHIPS, FLAT + 16, HD), BF16),
        pltpu.VMEM((PARTS, 2, CHIPS, GROUP, WIDE), BF16),
        pltpu.VMEM((ALL, FEAT), F32),
        pltpu.VMEM((KV, GROUP, FEAT), BF16),
        pltpu.VMEM((KV, GROUP, FEAT), BF16),
        dma((11,)),
        dma((2 * PARTS + 2,)),
        dma((2 * PARTS + 2,)),
        dma((PARTS, CHIPS)),
        dma((PARTS, CHIPS)),
        dma((CHIPS,)),
        dma((CHIPS,)),
        dma((CHIPS,)),
        dma((CHIPS,)),
        dma((PARTS, CHIPS)),
        dma((PARTS, CHIPS)),
        dma((PARTS, CHIPS)),
        dma((PARTS, CHIPS)),
        dma((PARTS, CHIPS)),
        dma((PARTS, CHIPS)),
        dma((PARTS, CHIPS)),
        dma((PARTS, CHIPS)),
        dma((PARTS, CHIPS)),
        dma((PARTS, CHIPS)),
        dma((KV,)),
        dma((KV,)),
    ]
    return pl.pallas_call(
        kernel,
        out_shape=(
            jax.ShapeDtypeStruct((PROMPT_G, FEAT), BF16),
            jax.ShapeDtypeStruct((STEPS, ROWS_G, FEAT), BF16),
        ),
        in_specs=[hbm] * 9 + [smem] * 2,
        out_specs=(vmem, vmem),
        scratch_shapes=scratch,
        compiler_params=pltpu.CompilerParams(
            collective_id=0, has_side_effects=True, vmem_limit_bytes=58 * 2**20
        ),
    )(
        prompt_in.reshape(CHIPS, PROMPT_G, FEAT),
        step_in.reshape(STEPS, CHIPS, ROWS_G, FEAT),
        norm_gain.reshape(1, FEAT),
        query_weight,
        key_weight,
        value_weight,
        out_weight,
        key_cache.reshape(SLOTS, HD),
        value_cache.reshape(SLOTS, HD),
        cache_lengths,
        visible,
    )


def solution(mesh):
    placed = (
        P(None, "ctx"),
        P(None, None, "ctx"),
        P("ctx"),
        P("ctx", "kv"),
        P("ctx", "kv"),
        P("ctx", "kv"),
        P("kv", "ctx"),
        P("kv", "ctx", None),
        P("kv", "ctx", None),
        P("ctx"),
        P(),
    )
    return jax.shard_map(
        on_device,
        mesh=mesh,
        in_specs=placed,
        out_specs=(P("kv", "ctx"), P(None, "kv", "ctx")),
        check_vma=False,
    )
```

time: 1040 us -> 89.3 us (0.09)
  waiting for transfers between devices: 678 us -> 0 us
  matrix products: 133 us -> 0 us
  blocking collectives: 115 us -> 0 us
  other arithmetic: 90.4 us -> 0 us
  Pallas kernels: 0 us -> 82.5 us
  between operations: 16.3 us -> 1.29 us
    reduce_scatter x4 -> x0, waiting for transfers between devices: 281 us -> none  [run_section(): lax.psum_scatter(jnp.einsum('srk,kd->rsd', attended, out_weight, preferre...]
    psum x2 -> x0, waiting for transfers between devices: 217 us -> none  [the longest x1 126 us: run_section(): query_sum, square_sum = lax.psum((query_part, squares), 'ctx')]
    unnamed x10 -> x0, waiting for transfers between devices: 180 us -> none
    dot_general x40 -> x0, matrix products: 133 us -> none  [the longest x7 71.2 us: one_block(): jnp.einsum('fd,cd->fc', query_block, key_shard, preferred_element_type=jn...]
    pallas_call x0 -> x1, Pallas kernels: none -> 82.5 us  [on_device(): pl.pallas_call(kernel, out_shape=(jax.ShapeDtypeStruct((PROMPT_G, FEAT),...]
    reduce_sum x14 -> x0, other arithmetic: 72.2 us -> none  [the longest x5 69.8 us: one_block(): jnp.sum(cache_weights, axis=1, dtype=jnp.float32)]
    psum x2 -> x0, blocking collectives: 58.8 us -> none  [the longest x1 31 us: run_section(): query_sum, square_sum = lax.psum((query_part, squares), 'ctx')]
    pmax x1 -> x0, blocking collectives: 55.9 us -> none  [run_section(): overall = lax.pmax(highest, 'ctx')]
  transfers between devices with their start and end apart: 8 -> 0, of which waited for: 8 -> 0; matrix products, arithmetic and copies ran while one was open for 2% -> 0% of each run, Pallas kernels for 0% -> 0%
where the time goes in v1:
time: 89.3 us; the launch traced here: 87.8 us
  Pallas kernels  82.5 us (92%)
  local copies, waits for them, and re-layouts  3.98 us (4%)
  between operations  1.29 us (1%)
    pallas_call x1, Pallas kernels, on_device(): pl.pallas_call(kernel, out_shape=(jax.ShapeDtypeStruct((PROMPT_G, FEAT),...  82.5 us
    unnamed x2, local copies, waits for them, and re-layouts  2.72 us

profile of v1, /device:TPU:0, one launch (start us, length us, event | category | flops | bytes accessed | tf_op | source)
XLA Modules:
  0.0 87.8 jit_solution(2750518399245585852)
XLA Ops:
  1.3 1.3 %reshape.21.gain_ref = bf16[1,512]{1,0:T(2,128)(2,1)} reshape(bf16[512]{0:T(512)(128)(2,1)} %param.13) | data formatting | bytes 2048 | tf_op jit(solution)/shard_map/reshape | solution.py:705
  2.5 82.5 %shard_map.122 = (bf16[32,512]{1,0:T(8,128)(2,1)}, bf16[3,8,512]{2,1,0:T(8,128)(2,1)}) custom-call(bf16[8,32,512]{2,1,0:T(8,128)(2,1)} %bitcast.6, bf16[3,8,8,512]{3,2,1,0:T(8,128)(2,1)} %bitcast.7, bf16[1,512]{1,0:T(2,128)(2,1)} %reshape.21.gain_ref, bf16[512,1024]{1,0:T(8,128)(2,1)} %wq_hbm.1, bf16[512,128]{1,0:T(8,128)(2,1)} %wk_hbm.1, ...), custom_call_target="tpu_custom_call" | custom-call | tf_op jit(solution)/shard_map/pallas_call | solution.py:690
  85.1 1.4 %copy.16 = bf16[32,512]{1,0:T(8,128)(2,1)} copy(bf16[32,512]{1,0:T(8,128)(2,1)} %get-tuple-element.4) | data formatting | bytes 65536
  86.5 1.3 %copy.17 = bf16[3,8,512]{2,1,0:T(8,128)(2,1)} copy(bf16[3,8,512]{2,1,0:T(8,128)(2,1)} %get-tuple-element.5) | data formatting | bytes 49152

commit v2 on v1

v2 whole, which is shorter than its diff:
```python
import jax
import jax.numpy as jnp
from jax import lax
from jax.experimental import pallas as pl
from jax.experimental.pallas import tpu as pltpu
from jax.sharding import PartitionSpec as P

D = 8192
HD = 128
EPSILON = 1e-05
MESH = pl.DeviceIdType.MESH
F32 = jnp.float32
BF16 = jnp.bfloat16

CTX = 16
KV = 8
CHIPS = 8
PROMPT = 256
ROWS = 64
STEPS = 3
PROMPT_N = PROMPT // ROWS
GRANULES = PROMPT_N + STEPS
SUB = ROWS // CHIPS
OWN = GRANULES * SUB
ALL = GRANULES * ROWS
FEAT = 512
WIDE = 512
HEADS = WIDE // HD
FLAT = HEADS * SUB
HALF = CHIPS * FLAT
BLOCK = 2 * HALF
PACK = FLAT + 8
SLOTS = 8192
TILE = 512
TILES = SLOTS // TILE
LOG2E = 1.4426950408889634
HIDDEN = -1e30
FRONT = ((0, 2), (2, 2), (4, 3))
BACK = ((0, 2), (2, 2), (4, 1), (5, 2))
DIRECT_Q = (False, True, False)
DIRECT_A = (False, False, False, False)


def kernel(
    prompt_ref,
    step_ref,
    gain_ref,
    wq_hbm,
    wk_hbm,
    wv_hbm,
    wo_hbm,
    key_hbm,
    value_hbm,
    length_ref,
    visible_ref,
    prompt_out,
    step_out,
    x_raw,
    gain,
    xs,
    wq,
    wkv,
    wo,
    k_raw,
    k_t,
    v_x,
    kx_t,
    vx_x,
    bias,
    inv,
    po,
    kvp,
    a0_send,
    a0_recv,
    kv0_send,
    kv0_recv,
    sq0_send,
    sq0_recv,
    a1_send,
    a1_recv,
    kv1_send,
    kv1_recv,
    sq1_send,
    sq1_recv,
    q_all,
    s_buf,
    sx_buf,
    mx,
    mix_all,
    top_all,
    b0_send,
    b0_recv,
    b1_send,
    b1_recv,
    att,
    cp_send,
    cp_recv,
    cs_send,
    cs_recv,
    load_sem,
    a0_ss,
    a0_rs,
    b0_ss,
    b0_rs,
    a1_ss,
    a1_rs,
    kv1_ss,
    kv1_rs,
    sq1_ss,
    sq1_rs,
    qg_ss,
    qg_rs,
    qf_ss,
    qf_rs,
    b1_ss,
    b1_rs,
    ag_ss,
    ag_rs,
    af_ss,
    af_rs,
    c_ss,
    c_rs,
):
    c = lax.axis_index("ctx")
    k = lax.axis_index("kv")
    core = lax.rem(c, 2)
    j = lax.div(c, 2)
    other = 1 - core
    sib = (c + 1 - 2 * core, k)
    any_direct = any(DIRECT_Q) or any(DIRECT_A)

    def chip(jt):
        return (2 * jt + core, k)

    def cross(jt):
        return (2 * jt + other, k)

    def away(d):
        return lax.rem(j + d, CHIPS)

    def remote(src, dst, ss, rs, dev):
        return pltpu.make_async_remote_copy(
            src_ref=src, dst_ref=dst, send_sem=ss, recv_sem=rs, device_id=dev, device_id_type=MESH
        )

    loads = [
        pltpu.make_async_copy(prompt_ref, x_raw.at[0:PROMPT], load_sem.at[0]),
        pltpu.make_async_copy(step_ref, x_raw.at[PROMPT:ALL], load_sem.at[1]),
        pltpu.make_async_copy(gain_ref, gain, load_sem.at[2]),
    ]
    weights_load = pltpu.make_async_copy(wq_hbm, wq, load_sem.at[3])
    pair_loads = [
        pltpu.make_async_copy(wk_hbm, wkv.at[:, 0:HD], load_sem.at[4]),
        pltpu.make_async_copy(wv_hbm, wkv.at[:, HD : 2 * HD], load_sem.at[5]),
    ]
    key_load = pltpu.make_async_copy(key_hbm, k_raw, load_sem.at[6])
    value_load = pltpu.make_async_copy(value_hbm, v_x.at[:, 0:HD], load_sem.at[7])
    wo_load = pltpu.make_async_copy(wo_hbm, wo, load_sem.at[8])
    for copy in loads:
        copy.start()
    weights_load.start()
    for copy in pair_loads:
        copy.start()

    barrier = pltpu.get_barrier_semaphore()
    pl.semaphore_signal(barrier, inc=1, device_id=sib, device_id_type=MESH)
    for d in range(1, CHIPS):
        pl.semaphore_signal(barrier, inc=1, device_id=chip(away(d)), device_id_type=MESH)
        if any_direct:
            pl.semaphore_signal(barrier, inc=1, device_id=cross(away(d)), device_id_type=MESH)
        pl.semaphore_signal(
            barrier, inc=1, device_id=(c, lax.rem(k + d, KV)), device_id_type=MESH
        )

    eye_flat = lax.broadcasted_iota(jnp.int32, (FLAT, HD), 0) == lax.broadcasted_iota(
        jnp.int32, (FLAT, HD), 1
    )
    eye_own = lax.broadcasted_iota(jnp.int32, (OWN, HD), 0) == lax.broadcasted_iota(
        jnp.int32, (OWN, HD), 1
    )

    def as_row(eye, column):
        return jnp.sum(jnp.where(eye, column, 0.0), axis=0, keepdims=True)

    def as_column(eye, row):
        return jnp.sum(jnp.where(eye, row, 0.0), axis=1, keepdims=True)

    for copy in loads:
        copy.wait()
    xf = x_raw[...].astype(F32)
    xs[...] = (xf * gain[...].astype(F32).reshape(1, FEAT)).astype(BF16)
    squares = jnp.sum(xf * xf, axis=1, keepdims=True)
    for jt in range(CHIPS):
        sq0_send[jt] = as_row(
            eye_own,
            jnp.concatenate(
                [squares[g * ROWS + jt * SUB : g * ROWS + (jt + 1) * SUB] for g in range(GRANULES)],
                axis=0,
            ),
        )
    weights_load.wait()
    for copy in pair_loads:
        copy.wait()
    key_load.start()
    value_load.start()
    wo_load.start()

    def rows_of(part):
        return slice(part[0] * ROWS, (part[0] + part[1]) * ROWS)

    def first(f):
        rows = rows_of(FRONT[f])
        return remote(a0_send.at[rows], a0_recv.at[rows], a0_ss.at[f], a0_rs.at[f], sib)

    def project(rows, column):
        return jnp.dot(
            xs[rows], wq[:, pl.ds(pl.multiple_of(column, HD), WIDE)], preferred_element_type=F32
        )

    kv_first = remote(kv0_send, kv0_recv, a0_ss.at[len(FRONT)], a0_rs.at[len(FRONT)], sib)
    sq_first = remote(sq0_send, sq0_recv, a0_ss.at[len(FRONT) + 1], a0_rs.at[len(FRONT) + 1], sib)
    start_rows = rows_of(FRONT[0])
    later_rows = slice(start_rows.stop, ALL)
    a0_send[start_rows] = project(start_rows, other * WIDE).astype(BF16)
    pl.semaphore_wait(barrier, (3 if any_direct else 2) * CHIPS - (2 if any_direct else 1))
    sq_first.start()
    first(0).start()
    po[start_rows] = project(start_rows, core * WIDE)

    length = length_ref[0]

    def prepare_keys(t, carry):
        low = pl.multiple_of(t * TILE, TILE)
        live = (lax.broadcasted_iota(jnp.int32, (TILE, HD), 0) + low) < length
        keys = jnp.where(live, k_raw[pl.ds(low, TILE)].astype(F32), k_raw[0:1].astype(F32))
        k_t[:, pl.ds(low, TILE)] = keys.astype(BF16).T
        return carry

    def prepare_values(t, carry):
        low = pl.multiple_of(t * TILE, TILE)
        live = (lax.broadcasted_iota(jnp.int32, (TILE, HD), 0) + low) < length
        v_x[pl.ds(low, TILE), 0:HD] = jnp.where(
            live, v_x[pl.ds(low, TILE), 0:HD].astype(F32), 0.0
        ).astype(BF16)
        v_x[pl.ds(low, TILE), HD : 2 * HD] = jnp.where(live, 1.0, 0.0).astype(BF16)
        return carry

    def span(part):
        return pl.ds(part[0], part[1])

    def a1_copy(f, jt, slot):
        grans = span(FRONT[f])
        return remote(
            a1_send.at[jt, grans],
            a1_recv.at[slot, grans],
            a1_ss.at[f, jt],
            a1_rs.at[f, slot],
            chip(jt),
        )

    def kv1_copy(jt, slot):
        return remote(kv1_send.at[jt], kv1_recv.at[slot], kv1_ss.at[jt], kv1_rs.at[slot], chip(jt))

    def sq1_copy(jt, slot):
        return remote(sq1_send.at[jt], sq1_recv.at[slot], sq1_ss.at[jt], sq1_rs.at[slot], chip(jt))

    def spread(f):
        first(f).wait_recv()
        g0, count = FRONT[f]
        for g in range(g0, g0 + count):
            rows = slice(g * ROWS, (g + 1) * ROWS)
            total = po[rows] + a0_recv[rows].astype(F32)
            a1_send[:, g] = total.reshape(CHIPS, SUB, WIDE).astype(BF16)
        for d in range(1, CHIPS):
            a1_copy(f, away(d), j).start()

    def spread_squares():
        sq_first.wait_recv()
        sq1_send[...] = sq0_send[...] + sq0_recv[...]
        for d in range(1, CHIPS):
            sq1_copy(away(d), j).start()

    def spread_pairs():
        kv_first.wait_recv()
        kv1_send[...] = (kvp[...] + kv0_recv[...].astype(F32)).astype(BF16)
        for d in range(1, CHIPS):
            kv1_copy(away(d), j).start()

    def square_sums():
        square = sq1_send[j]
        for d in range(1, CHIPS):
            src = away(d)
            sq1_copy(src, src).wait_recv()
            square = square + sq1_recv[src]
        inverse = lax.rsqrt(square / D + EPSILON)
        inv[...] = jnp.broadcast_to(as_column(eye_own, inverse), (OWN, HD))

    def pair_sums():
        pair = kv1_send[j].astype(F32)
        for d in range(1, CHIPS):
            src = away(d)
            kv1_copy(src, src).wait_recv()
            pair = pair + kv1_recv[src].astype(F32)
        pair = pair.reshape(PROMPT_N * SUB, 2 * HD)
        split = PROMPT_N * SUB
        inv_steps = jnp.concatenate([inv[split:], jnp.zeros((2 * split - OWN, HD), F32)], axis=0)
        scale = jnp.where(core == 0, inv[0:split], inv_steps)
        blank = jnp.zeros((HD - split, HD), F32)
        new_keys = jnp.concatenate([pair[:, 0:HD] * scale, blank], axis=0)
        new_values = jnp.concatenate([pair[:, HD:] * scale, blank], axis=0)
        kx_t[...] = new_keys.T.astype(BF16)
        vx_x[:, 0:HD] = new_values.astype(BF16)
        vx_x[:, HD : 2 * HD] = jnp.ones((HD, HD), BF16)

    def q_at(f, column, slot):
        return q_all.at[span(FRONT[f]), column, slot]

    def q_copy(f, jt, slot):
        return remote(
            q_at(f, core, slot), q_at(f, core, slot), qg_ss.at[f, jt], qg_rs.at[f, slot], chip(jt)
        )

    def q_cross(f, jt):
        return remote(
            q_at(f, core, j), q_at(f, core, j), qf_ss.at[f, jt], qf_rs.at[f, j], cross(jt)
        )

    def q_forward(f, column, slot):
        return remote(
            q_at(f, column, slot), q_at(f, column, slot), qf_ss.at[f, slot], qf_rs.at[f, slot], sib
        )

    def query_sums(f):
        g0, count = FRONT[f]
        grans = span(FRONT[f])
        total = a1_send[j, grans].astype(F32)
        for d in range(1, CHIPS):
            src = away(d)
            a1_copy(f, src, src).wait_recv()
            total = total + a1_recv[src, grans].astype(F32)
        for i in range(count):
            g = g0 + i
            scale = inv[g * SUB : (g + 1) * SUB] * (HD**-0.5 * LOG2E)
            flat = jnp.concatenate(
                [total[i, :, h * HD : (h + 1) * HD] * scale for h in range(HEADS)], axis=0
            )
            q_all[g, core, j] = flat.astype(BF16)
        for d in range(1, CHIPS):
            q_copy(f, away(d), j).start()
            if DIRECT_Q[f]:
                q_cross(f, away(d)).start()
        q_forward(f, core, j).start()

    def forward_queries(f):
        for d in range(1, CHIPS):
            src = away(d)
            q_copy(f, src, src).wait_recv()
            if not DIRECT_Q[f]:
                q_forward(f, core, src).start()

    def await_queries(f):
        for slot in range(CHIPS):
            q_forward(f, other, slot).wait_recv()

    def prepare_bias():
        lane = lax.broadcasted_iota(jnp.int32, (SUB, HD), 1)
        sub = lax.broadcasted_iota(jnp.int32, (SUB, HD), 0)
        lane_sub = lax.rem(lane, SUB)
        lane_gran = lax.div(lane, SUB)
        position = lane_gran * ROWS + j * SUB + lane_sub
        key_row = j * SUB + lane_sub
        for jt in range(CHIPS):
            seen_by_row = jnp.zeros((SUB, HD), jnp.int32)
            for b in range(SUB):
                seen_by_row = jnp.where(sub == b, visible_ref[jt * SUB + b], seen_by_row)
            query_row = jt * SUB + sub
            for g in range(GRANULES):
                limit = g * ROWS + query_row + 1 if g < PROMPT_N else seen_by_row
                on_prompt = jnp.where((lane_gran < PROMPT_N) & (position < limit), 0.0, HIDDEN)
                if g < PROMPT_N:
                    on_steps = jnp.full((SUB, HD), HIDDEN, F32)
                else:
                    on_steps = jnp.where(
                        (lane_gran <= g - PROMPT_N) & (key_row == query_row), 0.0, HIDDEN
                    )
                bias[g, jt] = jnp.where(core == 0, on_prompt, on_steps)

    key_load.wait()
    lax.fori_loop(0, TILES // 4, prepare_keys, 0)
    spread(0)
    spread_squares()
    a0_send[later_rows] = project(later_rows, other * WIDE).astype(BF16)
    for f in range(1, len(FRONT)):
        first(f).start()
    pairs = jnp.dot(xs[...], wkv[...], preferred_element_type=F32)
    pairs = pairs.reshape(GRANULES, CHIPS, SUB, 2 * HD)
    for i in range(PROMPT_N):
        of_prompt = pairs[i]
        of_steps = pairs[PROMPT_N + i] if i < STEPS else jnp.zeros((CHIPS, SUB, 2 * HD), F32)
        kv0_send[:, i] = jnp.where(core == 0, of_steps, of_prompt).astype(BF16)
        kvp[:, i] = jnp.where(core == 0, of_prompt, of_steps)
    kv_first.start()
    po[later_rows] = project(later_rows, core * WIDE)
    spread_pairs()
    square_sums()
    query_sums(0)
    spread(1)
    prepare_bias()
    lax.fori_loop(TILES // 4, TILES, prepare_keys, 0)
    forward_queries(0)
    query_sums(1)
    spread(2)
    value_load.wait()
    lax.fori_loop(0, TILES, prepare_values, 0)
    pair_sums()
    await_queries(0)

    def lane_max(scores):
        high = scores[:, 0:HD]
        for u in range(1, scores.shape[1] // HD):
            high = jnp.maximum(high, scores[:, u * HD : (u + 1) * HD])
        return high

    def sweep(n_scores, top):
        if n_scores is not None:
            queries = q_all[n_scores].reshape(BLOCK, HD)
            mask = bias[n_scores].reshape(1, CHIPS, 1, SUB, HD)
        high = None
        mixed = None
        for t in range(TILES + 1):
            cols = slice(t * TILE, (t + 1) * TILE)
            if top is not None:
                old = s_buf[t] if t < TILES else sx_buf[...]
                weights = jnp.exp2(old - top).astype(BF16)
            if n_scores is not None:
                if t < TILES:
                    scores = jnp.dot(queries, k_t[:, cols], preferred_element_type=F32)
                    s_buf[t] = scores
                else:
                    scores = jnp.dot(queries, kx_t[...], preferred_element_type=F32)
                    scores = scores.reshape(2, CHIPS, HEADS, SUB, HD) + mask
                    scores = scores.reshape(BLOCK, HD)
                    sx_buf[...] = scores
                peak = lane_max(scores)
                high = peak if high is None else jnp.maximum(high, peak)
            if top is not None:
                values = v_x[cols] if t < TILES else vx_x[...]
                part = jnp.dot(weights, values, preferred_element_type=F32)
                mixed = part if mixed is None else mixed + part
        if n_scores is not None:
            mx[...] = high
        return mixed

    def split3(row):
        one = row.astype(BF16).astype(F32)
        two = (row - one).astype(BF16).astype(F32)
        return one, two, row - one - two

    def packed(mixture, top_row, total_row):
        sub = lax.broadcasted_iota(jnp.int32, (PACK - FLAT, HD), 0)
        stats = jnp.zeros((PACK - FLAT, HD), F32)
        for i, piece in enumerate(split3(top_row) + split3(total_row)):
            stats = jnp.where(sub == i, piece, stats)
        return jnp.concatenate([mixture, stats], axis=0).astype(BF16)

    def unpacked(packet):
        wide = packet.astype(F32)
        stats = wide[FLAT:]
        return (
            wide[0:FLAT],
            stats[0:1] + stats[1:2] + stats[2:3],
            stats[3:4] + stats[4:5] + stats[5:6],
        )

    def block_of(n, column, jt):
        rows = slice(jt * FLAT, (jt + 1) * FLAT)
        top_row = as_row(eye_flat, top_all[n, column, rows])
        total_row = as_row(eye_flat, mix_all[n, column, rows, HD:])
        return mix_all[n, column, rows, 0:HD], top_row, total_row

    def keep(n, mixed, top):
        mix_all[n] = mixed.reshape(2, HALF, 2 * HD)
        top_all[n] = jnp.broadcast_to(top, (BLOCK, HD)).reshape(2, HALF, HD)
        for jt in range(CHIPS):
            b0_send[n, jt] = packed(*block_of(n, other, jt))

    def b0_copy(b):
        grans = span(BACK[b])
        return remote(b0_send.at[grans], b0_recv.at[grans], b0_ss.at[b], b0_rs.at[b], sib)

    def b1_copy(b, jt, slot):
        grans = span(BACK[b])
        return remote(
            b1_send.at[jt, grans], b1_recv.at[slot, grans], b1_ss.at[b, jt], b1_rs.at[b, slot], chip(jt)
        )

    def merge_pair(b):
        b0_copy(b).wait_recv()
        g0, count = BACK[b]
        for g in range(g0, g0 + count):
            for jt in range(CHIPS):
                mix1, top1, tot1 = unpacked(b0_recv[g, jt])
                mix0, top0, tot0 = block_of(g, core, jt)
                top = jnp.maximum(top0, top1)
                w0 = jnp.exp2(top0 - top)
                w1 = jnp.exp2(top1 - top)
                mixture = mix0 * as_column(eye_flat, w0) + mix1 * as_column(eye_flat, w1)
                b1_send[jt, g] = packed(mixture, top, w0 * tot0 + w1 * tot1)
        for d in range(1, CHIPS):
            b1_copy(b, away(d), j).start()

    def att_at(b, column, slot):
        return att.at[column, span(BACK[b]), slot]

    def att_copy(b, jt, slot):
        return remote(
            att_at(b, core, slot), att_at(b, core, slot), ag_ss.at[b, jt], ag_rs.at[b, slot], chip(jt)
        )

    def att_cross(b, jt):
        return remote(
            att_at(b, core, j), att_at(b, core, j), af_ss.at[b, jt], af_rs.at[b, j], cross(jt)
        )

    def att_forward(b, column, slot):
        return remote(
            att_at(b, column, slot),
            att_at(b, column, slot),
            af_ss.at[b, slot],
            af_rs.at[b, slot],
            sib,
        )

    def merge_all(b):
        g0, count = BACK[b]
        for d in range(1, CHIPS):
            b1_copy(b, away(d), away(d)).wait_recv()
        for g in range(g0, g0 + count):
            pieces = [unpacked(b1_send[j, g])]
            for d in range(1, CHIPS):
                pieces.append(unpacked(b1_recv[away(d), g]))
            top = pieces[0][1]
            for piece in pieces[1:]:
                top = jnp.maximum(top, piece[1])
            shares = [jnp.exp2(piece[1] - top) for piece in pieces]
            total = shares[0] * pieces[0][2]
            for share, piece in zip(shares[1:], pieces[1:]):
                total = total + share * piece[2]
            result = jnp.zeros((FLAT, HD), F32)
            for share, piece in zip(shares, pieces):
                result = result + piece[0] * as_column(eye_flat, share)
            result = result * as_column(eye_flat, 1.0 / total)
            att[core, g, j] = jnp.concatenate(
                [result[h * SUB : (h + 1) * SUB] for h in range(HEADS)], axis=1
            ).astype(BF16)
        for d in range(1, CHIPS):
            att_copy(b, away(d), j).start()
            if DIRECT_A[b]:
                att_cross(b, away(d)).start()
        att_forward(b, core, j).start()

    def forward_attended(b):
        for d in range(1, CHIPS):
            src = away(d)
            att_copy(b, src, src).wait_recv()
            if not DIRECT_A[b]:
                att_forward(b, core, src).start()

    def await_attended(b):
        for slot in range(CHIPS):
            att_forward(b, other, slot).wait_recv()

    def out_part(g0, count, column):
        rows = att[column, g0 : g0 + count].astype(F32).reshape(count * ROWS, WIDE).astype(BF16)
        low = pl.multiple_of(column * WIDE, WIDE)
        return jnp.dot(rows, wo[pl.ds(low, WIDE)], preferred_element_type=F32)

    def cp_copy(kt, slot):
        return remote(cp_send.at[kt], cp_recv.at[slot], c_ss.at[0, kt], c_rs.at[0, slot], (c, kt))

    def cs_copy(kt, slot):
        return remote(cs_send.at[kt], cs_recv.at[slot], c_ss.at[1, kt], c_rs.at[1, slot], (c, kt))

    def next_kv(d):
        return lax.rem(k + d, KV)

    def finish_prompt():
        result = out_part(0, PROMPT_N, core) + out_part(0, PROMPT_N, other)
        cp_send[...] = result.reshape(KV, PROMPT // KV, FEAT).astype(BF16)
        for d in range(1, KV):
            cp_copy(next_kv(d), k).start()

    def finish_steps():
        result = out_part(PROMPT_N, STEPS, core) + out_part(PROMPT_N, STEPS, other)
        for s in range(STEPS):
            piece = result[s * ROWS : (s + 1) * ROWS]
            cs_send[:, s] = piece.reshape(KV, SUB, FEAT).astype(BF16)
        for d in range(1, KV):
            cs_copy(next_kv(d), k).start()

    def write_prompt():
        final = cp_send[k].astype(F32)
        for d in range(1, KV):
            src = next_kv(d)
            cp_copy(src, src).wait_recv()
            final = final + cp_recv[src].astype(F32)
        prompt_out[...] = final.astype(BF16)

    def write_steps():
        final = cs_send[k].astype(F32)
        for d in range(1, KV):
            src = next_kv(d)
            cs_copy(src, src).wait_recv()
            final = final + cs_recv[src].astype(F32)
        step_out[...] = final.astype(BF16)

    def step_top():
        return jnp.max(mx[...], axis=1, keepdims=True)

    sweep(0, None)

    def step(n, carry):
        @pl.when(n == 1)
        def _():
            forward_queries(1)
            query_sums(2)
            await_queries(1)

        @pl.when(n == 2)
        def _():
            b0_copy(0).start()
            forward_queries(2)

        @pl.when(n == 3)
        def _():
            await_queries(2)
            merge_pair(0)

        @pl.when(n == 4)
        def _():
            b0_copy(1).start()
            merge_all(0)

        @pl.when(n == 5)
        def _():
            b0_copy(2).start()
            merge_pair(1)
            forward_attended(0)

        top = step_top()
        keep(n, sweep(n + 1, top), top)
        return carry

    last = GRANULES - 1
    lax.fori_loop(0, last, step, 0)
    merge_pair(2)
    merge_all(1)
    top = step_top()
    keep(last, sweep(None, top), top)
    b0_copy(3).start()
    merge_all(2)
    forward_attended(1)
    merge_pair(3)
    await_attended(0)
    await_attended(1)
    wo_load.wait()
    finish_prompt()
    forward_attended(2)
    merge_all(3)
    forward_attended(3)
    write_prompt()
    await_attended(2)
    await_attended(3)
    finish_steps()
    write_steps()

    kv_first.wait_send()
    sq_first.wait_send()
    for f in range(len(FRONT)):
        first(f).wait_send()
        q_forward(f, core, j).wait_send()
    for b in range(len(BACK)):
        b0_copy(b).wait_send()
        att_forward(b, core, j).wait_send()
    for d in range(1, CHIPS):
        jt = away(d)
        sq1_copy(jt, j).wait_send()
        kv1_copy(jt, j).wait_send()
        cp_copy(next_kv(d), k).wait_send()
        cs_copy(next_kv(d), k).wait_send()
        for f in range(len(FRONT)):
            a1_copy(f, jt, j).wait_send()
            q_copy(f, jt, j).wait_send()
            if DIRECT_Q[f]:
                q_cross(f, jt).wait_send()
            else:
                q_forward(f, core, jt).wait_send()
        for b in range(len(BACK)):
            b1_copy(b, jt, j).wait_send()
            att_copy(b, jt, j).wait_send()
            if DIRECT_A[b]:
                att_cross(b, jt).wait_send()
            else:
                att_forward(b, core, jt).wait_send()


def place_outputs(prompt_ref, step_ref, prompt_out, step_out):
    prompt_out[...] = prompt_ref[...]
    step_out[...] = step_ref[...]


def on_device(
    prompt_in,
    step_in,
    norm_gain,
    query_weight,
    key_weight,
    value_weight,
    out_weight,
    key_cache,
    value_cache,
    cache_lengths,
    visible,
):
    dma = pltpu.SemaphoreType.DMA
    hbm = pl.BlockSpec(memory_space=pl.ANY)
    smem = pl.BlockSpec(memory_space=pltpu.SMEM)
    vmem = pl.BlockSpec(memory_space=pltpu.VMEM)
    fronts, backs = len(FRONT), len(BACK)
    scratch = [
        pltpu.VMEM((ALL, FEAT), BF16),
        pltpu.VMEM((FEAT,), BF16),
        pltpu.VMEM((ALL, FEAT), BF16),
        pltpu.VMEM((FEAT, 2 * WIDE), BF16),
        pltpu.VMEM((FEAT, 2 * HD), BF16),
        pltpu.VMEM((2 * WIDE, FEAT), BF16),
        pltpu.VMEM((SLOTS, HD), BF16),
        pltpu.VMEM((HD, SLOTS), BF16),
        pltpu.VMEM((SLOTS, 2 * HD), BF16),
        pltpu.VMEM((HD, HD), BF16),
        pltpu.VMEM((HD, 2 * HD), BF16),
        pltpu.VMEM((GRANULES, CHIPS, SUB, HD), F32),
        pltpu.VMEM((OWN, HD), F32),
        pltpu.VMEM((ALL, WIDE), F32),
        pltpu.VMEM((CHIPS, PROMPT_N, SUB, 2 * HD), F32),
        pltpu.VMEM((ALL, WIDE), BF16),
        pltpu.VMEM((ALL, WIDE), BF16),
        pltpu.VMEM((CHIPS, PROMPT_N, SUB, 2 * HD), BF16),
        pltpu.VMEM((CHIPS, PROMPT_N, SUB, 2 * HD), BF16),
        pltpu.VMEM((CHIPS, 1, HD), F32),
        pltpu.VMEM((CHIPS, 1, HD), F32),
        pltpu.VMEM((CHIPS, GRANULES, SUB, WIDE), BF16),
        pltpu.VMEM((CHIPS, GRANULES, SUB, WIDE), BF16),
        pltpu.VMEM((CHIPS, PROMPT_N, SUB, 2 * HD), BF16),
        pltpu.VMEM((CHIPS, PROMPT_N, SUB, 2 * HD), BF16),
        pltpu.VMEM((CHIPS, 1, HD), F32),
        pltpu.VMEM((CHIPS, 1, HD), F32),
        pltpu.VMEM((GRANULES, 2, CHIPS, FLAT, HD), BF16),
        pltpu.VMEM((TILES, BLOCK, TILE), F32),
        pltpu.VMEM((BLOCK, HD), F32),
        pltpu.VMEM((BLOCK, HD), F32),
        pltpu.VMEM((GRANULES, 2, HALF, 2 * HD), F32),
        pltpu.VMEM((GRANULES, 2, HALF, HD), F32),
        pltpu.VMEM((GRANULES, CHIPS, PACK, HD), BF16),
        pltpu.VMEM((GRANULES, CHIPS, PACK, HD), BF16),
        pltpu.VMEM((CHIPS, GRANULES, PACK, HD), BF16),
        pltpu.VMEM((CHIPS, GRANULES, PACK, HD), BF16),
        pltpu.VMEM((2, GRANULES, CHIPS, SUB, WIDE), BF16),
        pltpu.VMEM((KV, PROMPT // KV, FEAT), BF16),
        pltpu.VMEM((KV, PROMPT // KV, FEAT), BF16),
        pltpu.VMEM((KV, STEPS, SUB, FEAT), BF16),
        pltpu.VMEM((KV, STEPS, SUB, FEAT), BF16),
        dma((9,)),
        dma((fronts + 2,)),
        dma((fronts + 2,)),
        dma((backs,)),
        dma((backs,)),
        dma((fronts, CHIPS)),
        dma((fronts, CHIPS)),
        dma((CHIPS,)),
        dma((CHIPS,)),
        dma((CHIPS,)),
        dma((CHIPS,)),
        dma((fronts, CHIPS)),
        dma((fronts, CHIPS)),
        dma((fronts, CHIPS)),
        dma((fronts, CHIPS)),
        dma((backs, CHIPS)),
        dma((backs, CHIPS)),
        dma((backs, CHIPS)),
        dma((backs, CHIPS)),
        dma((backs, CHIPS)),
        dma((backs, CHIPS)),
        dma((2, KV)),
        dma((2, KV)),
    ]
    shapes = (
        jax.ShapeDtypeStruct((PROMPT // KV, FEAT), BF16),
        jax.ShapeDtypeStruct((STEPS, SUB, FEAT), BF16),
    )
    results = pl.pallas_call(
        kernel,
        out_shape=shapes,
        in_specs=[hbm] * 9 + [smem] * 2,
        out_specs=(vmem, vmem),
        scratch_shapes=scratch,
        compiler_params=pltpu.CompilerParams(
            collective_id=0, has_side_effects=True, vmem_limit_bytes=58 * 2**20
        ),
    )(
        prompt_in,
        step_in.reshape(STEPS * ROWS, FEAT),
        norm_gain,
        query_weight,
        key_weight,
        value_weight,
        out_weight,
        key_cache.reshape(SLOTS, HD),
        value_cache.reshape(SLOTS, HD),
        cache_lengths,
        visible,
    )
    return pl.pallas_call(
        place_outputs, out_shape=shapes, in_specs=[vmem] * 2, out_specs=(vmem, vmem)
    )(*results)


def solution(mesh):
    placed = (
        P(None, "ctx"),
        P(None, None, "ctx"),
        P("ctx"),
        P("ctx", "kv"),
        P("ctx", "kv"),
        P("ctx", "kv"),
        P("kv", "ctx"),
        P("kv", "ctx", None),
        P("kv", "ctx", None),
        P("ctx"),
        P(),
    )
    return jax.shard_map(
        on_device,
        mesh=mesh,
        in_specs=placed,
        out_specs=(P("kv", "ctx"), P(None, "kv", "ctx")),
        check_vma=False,
    )
```

time: 89.3 us -> 83.7 us (0.937)
  local copies, waits for them, and re-layouts: 3.98 us -> 0 us
  Pallas kernels: 82.5 us -> 80.9 us
    unnamed x2 -> x0, local copies, waits for them, and re-layouts: 2.72 us -> none
    pallas_call x1 -> x2, Pallas kernels: 82.5 us -> 80.9 us  [the longest x1 79.5 us: on_device(): pl.pallas_call(kernel, out_shape=shapes, in_specs=[hbm] * 9 + [smem] * 2,...]
    reshape x1 -> x0, local copies, waits for them, and re-layouts: 1.26 us -> none  [on_device(): norm_gain.reshape(1, FEAT)]
where the time goes in v2:
time: 83.7 us; the launch traced here: 82.2 us
  Pallas kernels  80.9 us (97%)
  between operations  1.29 us (2%)
    pallas_call x1, Pallas kernels, on_device(): pl.pallas_call(kernel, out_shape=shapes, in_specs=[hbm] * 9 + [smem] * 2,...  79.5 us

profile of v2, /device:TPU:0, one launch (start us, length us, event | category | flops | bytes accessed | tf_op | source)
XLA Modules:
  0.0 82.2 jit_solution(8891724956908398795)
XLA Ops:
  1.3 79.5 %shard_map.122 = (bf16[32,512]{1,0:T(8,128)(2,1)}, bf16[3,8,512]{2,1,0:T(8,128)(2,1)}) custom-call(bf16[256,512]{1,0:T(8,128)(2,1)} %prompt_ref.1, bf16[192,512]{1,0:T(8,128)(2,1)} %bitcast.5, bf16[512]{0:T(512)(128)(2,1)} %gain_ref.1, bf16[512,1024]{1,0:T(8,128)(2,1)} %wq_hbm.1, bf16[512,128]{1,0:T(8,128)(2,1)} %wk_hbm.1, bf16[512,128]{1,0:T(8,128)(2,1)} %wv_hbm.1, ...), custom_call_target="tpu_custom_call" | custom-call | tf_op jit(solution)/shard_map/pallas_call | solution.py:801
  80.8 1.4 %shard_map.123 = (bf16[32,512]{1,0:T(8,128)(2,1)}, bf16[3,8,512]{2,1,0:T(8,128)(2,1)}) custom-call(bf16[32,512]{1,0:T(8,128)(2,1)} %get-tuple-element.4.prompt_ref, bf16[3,8,512]{2,1,0:T(8,128)(2,1)} %get-tuple-element.5.step_ref), custom_call_target="tpu_custom_call" | custom-call | tf_op jit(solution)/shard_map/pallas_call | solution.py:823

commit v3 on v2

--- a/solution.py
+++ b/solution.py
@@ -36,9 +36,9 @@
 LOG2E = 1.4426950408889634
 HIDDEN = -1e30
 FRONT = ((0, 2), (2, 2), (4, 3))
-BACK = ((0, 2), (2, 2), (4, 1), (5, 2))
-DIRECT_Q = (False, True, False)
-DIRECT_A = (False, False, False, False)
+BACK = ((0, 2), (2, 2), (4, 1), (5, 1), (6, 1))
+DIRECT_Q = (False, False, False)
+DIRECT_A = (False, False, False, False, False)
 
 
 def kernel(
@@ -385,8 +385,6 @@
                     )
                 bias[g, jt] = jnp.where(core == 0, on_prompt, on_steps)
 
-    key_load.wait()
-    lax.fori_loop(0, TILES // 4, prepare_keys, 0)
     spread(0)
     spread_squares()
     a0_send[later_rows] = project(later_rows, other * WIDE).astype(BF16)
@@ -401,17 +399,19 @@
         kvp[:, i] = jnp.where(core == 0, of_prompt, of_steps)
     kv_first.start()
     po[later_rows] = project(later_rows, core * WIDE)
-    spread_pairs()
+    spread(1)
     square_sums()
     query_sums(0)
-    spread(1)
+    spread_pairs()
     prepare_bias()
-    lax.fori_loop(TILES // 4, TILES, prepare_keys, 0)
-    forward_queries(0)
+    key_load.wait()
+    lax.fori_loop(0, TILES // 2, prepare_keys, 0)
     query_sums(1)
     spread(2)
+    lax.fori_loop(TILES // 2, TILES, prepare_keys, 0)
     value_load.wait()
     lax.fori_loop(0, TILES, prepare_values, 0)
+    forward_queries(0)
     pair_sums()
     await_queries(0)
 
@@ -578,8 +578,15 @@
     def cp_copy(kt, slot):
         return remote(cp_send.at[kt], cp_recv.at[slot], c_ss.at[0, kt], c_rs.at[0, slot], (c, kt))
 
-    def cs_copy(kt, slot):
-        return remote(cs_send.at[kt], cs_recv.at[slot], c_ss.at[1, kt], c_rs.at[1, slot], (c, kt))
+    def cs_copy(low, high, kt, slot):
+        i = 1 if low == 0 else 2
+        return remote(
+            cs_send.at[kt, low:high],
+            cs_recv.at[slot, low:high],
+            c_ss.at[i, kt],
+            c_rs.at[i, slot],
+            (c, kt),
+        )
 
     def next_kv(d):
         return lax.rem(k + d, KV)
@@ -590,13 +597,14 @@
         for d in range(1, KV):
             cp_copy(next_kv(d), k).start()
 
-    def finish_steps():
-        result = out_part(PROMPT_N, STEPS, core) + out_part(PROMPT_N, STEPS, other)
-        for s in range(STEPS):
+    def finish_steps(low, high):
+        count = high - low
+        result = out_part(PROMPT_N + low, count, core) + out_part(PROMPT_N + low, count, other)
+        for s in range(count):
             piece = result[s * ROWS : (s + 1) * ROWS]
-            cs_send[:, s] = piece.reshape(KV, SUB, FEAT).astype(BF16)
+            cs_send[:, low + s] = piece.reshape(KV, SUB, FEAT).astype(BF16)
         for d in range(1, KV):
-            cs_copy(next_kv(d), k).start()
+            cs_copy(low, high, next_kv(d), k).start()
 
     def write_prompt():
         final = cp_send[k].astype(F32)
@@ -606,24 +614,24 @@
             final = final + cp_recv[src].astype(F32)
         prompt_out[...] = final.astype(BF16)
 
-    def write_steps():
-        final = cs_send[k].astype(F32)
+    def write_steps(low, high):
+        final = cs_send[k, low:high].astype(F32)
         for d in range(1, KV):
             src = next_kv(d)
-            cs_copy(src, src).wait_recv()
-            final = final + cs_recv[src].astype(F32)
-        step_out[...] = final.astype(BF16)
+            cs_copy(low, high, src, src).wait_recv()
+            final = final + cs_recv[src, low:high].astype(F32)
+        step_out[low:high] = final.astype(BF16)
 
     def step_top():
         return jnp.max(mx[...], axis=1, keepdims=True)
 
     sweep(0, None)
+    forward_queries(1)
+    query_sums(2)
 
     def step(n, carry):
         @pl.when(n == 1)
         def _():
-            forward_queries(1)
-            query_sums(2)
             await_queries(1)
 
         @pl.when(n == 2)
@@ -653,26 +661,33 @@
 
     last = GRANULES - 1
     lax.fori_loop(0, last, step, 0)
+    b0_copy(3).start()
     merge_pair(2)
     merge_all(1)
     top = step_top()
     keep(last, sweep(None, top), top)
-    b0_copy(3).start()
+    b0_copy(4).start()
+    merge_pair(3)
+    merge_pair(4)
     merge_all(2)
     forward_attended(1)
-    merge_pair(3)
     await_attended(0)
     await_attended(1)
+    merge_all(3)
+    merge_all(4)
     wo_load.wait()
     finish_prompt()
     forward_attended(2)
-    merge_all(3)
     forward_attended(3)
-    write_prompt()
     await_attended(2)
     await_attended(3)
-    finish_steps()
-    write_steps()
+    finish_steps(0, STEPS - 1)
+    forward_attended(4)
+    await_attended(4)
+    finish_steps(STEPS - 1, STEPS)
+    write_prompt()
+    write_steps(0, STEPS - 1)
+    write_steps(STEPS - 1, STEPS)
 
     kv_first.wait_send()
     sq_first.wait_send()
@@ -687,7 +702,8 @@
         sq1_copy(jt, j).wait_send()
         kv1_copy(jt, j).wait_send()
         cp_copy(next_kv(d), k).wait_send()
-        cs_copy(next_kv(d), k).wait_send()
+        cs_copy(0, STEPS - 1, next_kv(d), k).wait_send()
+        cs_copy(STEPS - 1, STEPS, next_kv(d), k).wait_send()
         for f in range(len(FRONT)):
             a1_copy(f, jt, j).wait_send()
             q_copy(f, jt, j).wait_send()
@@ -791,8 +807,8 @@
         dma((backs, CHIPS)),
         dma((backs, CHIPS)),
         dma((backs, CHIPS)),
-        dma((2, KV)),
-        dma((2, KV)),
+        dma((3, KV)),
+        dma((3, KV)),
     ]
     shapes = (
         jax.ShapeDtypeStruct((PROMPT // KV, FEAT), BF16),

time: 83.7 us -> 80.9 us (0.967); the launches traced: 82.2 us -> 80.7 us
  Pallas kernels: 80.9 us -> 79.4 us
    pallas_call x1, Pallas kernels: 79.5 us -> 78 us  [on_device(): pl.pallas_call(kernel, out_shape=shapes, in_specs=[hbm] * 9 + [smem] * 2,...]
where the time goes in v3:
time: 80.9 us; the launch traced here: 80.7 us
  Pallas kernels  79.4 us (98%)
  between operations  1.29 us (2%)
    pallas_call x1, Pallas kernels, on_device(): pl.pallas_call(kernel, out_shape=shapes, in_specs=[hbm] * 9 + [smem] * 2,...  78 us

profile of v3, /device:TPU:0, one launch (start us, length us, event | category | flops | bytes accessed | tf_op | source)
XLA Modules:
  0.0 80.7 jit_solution(15626232957597618502)
XLA Ops:
  1.3 78.0 %shard_map.122 = (bf16[32,512]{1,0:T(8,128)(2,1)}, bf16[3,8,512]{2,1,0:T(8,128)(2,1)}) custom-call(bf16[256,512]{1,0:T(8,128)(2,1)} %prompt_ref.1, bf16[192,512]{1,0:T(8,128)(2,1)} %bitcast.5, bf16[512]{0:T(512)(128)(2,1)} %gain_ref.1, bf16[512,1024]{1,0:T(8,128)(2,1)} %wq_hbm.1, bf16[512,128]{1,0:T(8,128)(2,1)} %wk_hbm.1, bf16[512,128]{1,0:T(8,128)(2,1)} %wv_hbm.1, ...), custom_call_target="tpu_custom_call" | custom-call | tf_op jit(solution)/shard_map/pallas_call | solution.py:817
  79.3 1.4 %shard_map.123 = (bf16[32,512]{1,0:T(8,128)(2,1)}, bf16[3,8,512]{2,1,0:T(8,128)(2,1)}) custom-call(bf16[32,512]{1,0:T(8,128)(2,1)} %get-tuple-element.4.prompt_ref, bf16[3,8,512]{2,1,0:T(8,128)(2,1)} %get-tuple-element.5.step_ref), custom_call_target="tpu_custom_call" | custom-call | tf_op jit(solution)/shard_map/pallas_call | solution.py:839
